TPU v7x, 256 devices: a whole 4x4x8 slice. The times are simulated.
256 devices in a mesh: dp: 4 (over x), tm: 16 (over z, core), head: 4 (over y).
Axes of the slice: x: 4, y: 4, z: 8, core: 2. Of those that a mesh axis runs over, the one named last changes fastest.
Arguments:
- query_in: bfloat16 [4, 1024, 1280], P('dp', 'tm'), may hold values from -60 to 60
- grad_out: bfloat16 [4, 1024, 1280], P('dp', 'tm'), may hold values from -6 to 6
- encoder_states: bfloat16 [4, 4096, 1280], P('dp', 'tm'), may hold values from -24 to 24
- frame_lengths: int32 [4], P('dp'), may hold values from 2048 to 4096, as said below
- w_query: bfloat16 [1280, 1280], P(None, 'head'), may hold values from -0.15625 to 0.15625
- w_key: bfloat16 [1280, 1280], P(None, 'head'), may hold values from -0.15625 to 0.15625
- w_value: bfloat16 [1280, 1280], P(None, 'head'), may hold values from -0.15625 to 0.15625
- w_out: bfloat16 [1280, 1280], P('head'), may hold values from -0.15625 to 0.15625
Outputs:
- grad_query_in: bfloat16 [4, 1024, 1280], P('dp', 'tm', 'head')
- grad_encoder: bfloat16 [4, 4096, 1280], P('dp', 'tm', 'head')
- grad_w_query: float32 [1280, 1280], P(('dp', 'tm'), 'head')
- grad_w_key: float32 [1280, 1280], P(('dp', 'tm'), 'head')
- grad_w_value: float32 [1280, 1280], P(('dp', 'tm'), 'head')
- grad_w_out: float32 [1280, 1280], P('head', ('dp', 'tm'))
Inputs may be any that keep to these rules, and one draw needn't show every extreme that they name: `frame_lengths`: multiples of 128; some recording has all 4096 frames valid and another exactly half of them.
All inputs are finite; a program needn't handle non-finite values.
Results may differ from a plain program's by a relative error of at most 0.024.
The roundings to bfloat16 on the way count: a program that leaves them out, or rounds other values in their place, can miss the bound.
Values may be sent and summed in bfloat16 or wider, within the bound.
No kernel may reach another device: no remote copies, remote signals or barrier semaphores. Data moves between devices by JAX's collectives and lax.ppermute only.
A program may use at most 128 MiB of HBM per device.

v0:
```python
import jax
import jax.numpy as jnp
from jax import lax
from jax.sharding import PartitionSpec as P

HD = 64


def per_device(query_in, grad_out, encoder_states, frame_lengths, w_query, w_key, w_value, w_out):
    query_rows = query_in[0]
    dout_rows = grad_out[0]
    frames = encoder_states[0]
    head_count = w_query.shape[1] // HD
    score_scale = HD ** (-0.5)
    local_rows = query_rows.shape[0]
    slab_rows = frames.shape[0]
    query_part = jnp.dot(query_rows, w_query, preferred_element_type=jnp.float32).astype(
        jnp.bfloat16
    )
    dout_part = jnp.dot(dout_rows, w_out.T, preferred_element_type=jnp.float32).astype(jnp.bfloat16)
    query_all, dout_all = (
        lax.all_gather(query_part, "tm", axis=0, tiled=True),
        lax.all_gather(dout_part, "tm", axis=0, tiled=True),
    )
    total_rows = query_all.shape[0]
    keys = jnp.dot(frames, w_key, preferred_element_type=jnp.float32).astype(jnp.bfloat16)
    values = jnp.dot(frames, w_value, preferred_element_type=jnp.float32).astype(jnp.bfloat16)
    slab_index = lax.axis_index("tm")
    positions = slab_index * slab_rows + jnp.arange(slab_rows, dtype=jnp.int32)
    frame_mask = positions < frame_lengths[0]
    query_heads = query_all.reshape(total_rows, head_count, HD)
    dout_heads = dout_all.reshape(total_rows, head_count, HD)
    key_heads = keys.reshape(slab_rows, head_count, HD)
    value_heads = values.reshape(slab_rows, head_count, HD)
    scores = (
        jnp.einsum("qhd,fhd->hqf", query_heads, key_heads, preferred_element_type=jnp.float32)
        * score_scale
    )
    scores = jnp.where(frame_mask[None, None, :], scores, -1e30)
    local_top = jnp.max(scores, axis=2)
    value_float = value_heads.astype(jnp.float32)
    row_top = lax.pmax(local_top, "tm")
    weights_exp = jnp.where(frame_mask[None, None, :], jnp.exp(scores - row_top[..., None]), 0.0)
    local_sum = jnp.sum(weights_exp, axis=2)
    local_out = jnp.einsum(
        "hqf,fhd->hqd", weights_exp, value_float, precision=lax.Precision.HIGHEST
    )
    row_sum, out_sum = lax.psum((local_sum, local_out), "tm")
    probs = weights_exp / row_sum[..., None]
    attended = out_sum / row_sum[..., None]
    dout_float = jnp.transpose(dout_heads.astype(jnp.float32), (1, 0, 2))
    row_delta = jnp.sum(dout_float * attended, axis=2)
    dprobs = jnp.einsum("qhd,fhd->hqf", dout_heads, value_heads, preferred_element_type=jnp.float32)
    dscores = (probs * (dprobs - row_delta[..., None])).astype(jnp.bfloat16)
    probs_low = probs.astype(jnp.bfloat16)
    dquery_part = (
        jnp.einsum("hqf,fhd->qhd", dscores, key_heads, preferred_element_type=jnp.float32)
        * score_scale
    )
    dquery_part = dquery_part.reshape(total_rows, head_count * HD)
    dquery = lax.psum_scatter(
        dquery_part.astype(jnp.bfloat16), "tm", scatter_dimension=0, tiled=True
    )
    dkey = (
        jnp.einsum("hqf,qhd->fhd", dscores, query_heads, preferred_element_type=jnp.float32)
        * score_scale
    ).astype(jnp.bfloat16)
    dkey = dkey.reshape(slab_rows, head_count * HD)
    dvalue = jnp.einsum(
        "hqf,qhd->fhd", probs_low, dout_heads, preferred_element_type=jnp.float32
    ).astype(jnp.bfloat16)
    dvalue = dvalue.reshape(slab_rows, head_count * HD)
    dinput_part = jnp.dot(dquery, w_query.T, preferred_element_type=jnp.float32)
    dinput = lax.psum_scatter(
        dinput_part.astype(jnp.bfloat16), "head", scatter_dimension=1, tiled=True
    )
    frame_term = jnp.dot(dkey, w_key.T, preferred_element_type=jnp.float32) + jnp.dot(
        dvalue, w_value.T, preferred_element_type=jnp.float32
    )
    dframes = lax.psum_scatter(
        frame_term.astype(jnp.bfloat16), "head", scatter_dimension=1, tiled=True
    )
    attended_all = jnp.transpose(attended, (1, 0, 2)).reshape(total_rows, head_count * HD)
    attended_rows = lax.dynamic_slice_in_dim(
        attended_all, slab_index * local_rows, local_rows, 0
    ).astype(jnp.bfloat16)
    grad_query_w = jnp.dot(query_rows.T, dquery, preferred_element_type=jnp.float32)
    grad_key_w = jnp.dot(frames.T, dkey, preferred_element_type=jnp.float32)
    grad_value_w = jnp.dot(frames.T, dvalue, preferred_element_type=jnp.float32)
    grad_out_w = jnp.dot(dout_rows.T, attended_rows, preferred_element_type=jnp.float32)
    summed_q, summed_k, summed_v, summed_o = (
        lax.psum_scatter(grad_query_w, ("dp", "tm"), scatter_dimension=0, tiled=True),
        lax.psum_scatter(grad_key_w, ("dp", "tm"), scatter_dimension=0, tiled=True),
        lax.psum_scatter(grad_value_w, ("dp", "tm"), scatter_dimension=0, tiled=True),
        lax.psum_scatter(grad_out_w, ("dp", "tm"), scatter_dimension=0, tiled=True),
    )
    return (dinput[None], dframes[None], summed_q, summed_k, summed_v, summed_o.T)


def solution(mesh):
    placed = (
        P("dp", "tm", None),
        P("dp", "tm", None),
        P("dp", "tm", None),
        P("dp"),
        P(None, "head"),
        P(None, "head"),
        P(None, "head"),
        P("head", None),
    )
    return jax.shard_map(
        per_device,
        mesh=mesh,
        in_specs=placed,
        out_specs=(
            P("dp", "tm", "head"),
            P("dp", "tm", "head"),
            P(("dp", "tm"), "head"),
            P(("dp", "tm"), "head"),
            P(("dp", "tm"), "head"),
            P("head", ("dp", "tm")),
        ),
        check_vma=False,
    )
```

profile of v0, /device:TPU:8, one launch (start us, length us, event | category | flops | bytes accessed | tf_op | source)
XLA Modules:
  0.0 531.9 jit_solution(12440687611186662010)
XLA Ops:
  7.2 0.0 all-reduce.8.cloned.1.call-start
  7.2 1.1 copy-done
  8.3 1.5 convolution_convert_fusion.2
  9.8 1.8 convolution_convert_fusion.1
  12.2 1.6 convolution_convert_fusion.4
  13.8 22.1 %all_gather.6 = bf16[1024,320]{1,0:T(8,128)(2,1)S(1)} all-gather(bf16[64,320]{1,0:T(8,128)(2,1)S(1)} %convolution_convert_fusion.4), channel_id=1, replica_groups=mesh['dp'=4,'tm'=16,'head'=4] {'tm'}, dimensions={0}, use_global_device_ids=true | all-gather | bytes 696320 | tf_op jit(solution)/shard_map/all_gather | solution.py:22
  36.0 0.3 copy.39
  36.3 3.3 fusion
  39.6 45.9 %pmax.7 = f32[5,1024]{1,0:T(8,128)S(1)} all-reduce(f32[5,1024]{1,0:T(8,128)S(1)} %get-tuple-element.30), channel_id=1, replica_groups=mesh['dp'=4,'tm'=16,'head'=4] {'tm'}, use_global_device_ids=true, to_apply=%region_1.2 | all-reduce | flops 5120 | bytes 40960 | tf_op jit(solution)/shard_map/pmax | solution.py:42
  85.5 6.9 %fusion.19 = f32[5,1024,64]{1,2,0:T(8,128)} fusion(bf16[256,5,64]{0,2,1:T(8,128)(2,1)S(1)} %bitcast.102, f32[5,1024,256]{1,2,0:T(8,128)} %get-tuple-element.31, f32[5,1024]{1,0:T(8,128)S(1)} %pmax.7, pred[256]{0:T(512)(128)(4,1)S(1)} %add_compare_fusion), kind=kOutput, calls=%fused_computation.41 | convolution fusion | flops 1011875840 | bytes 6738176 | tf_op jit(solution)/shard_map/hqf,fhd->hqd/dot_general | solution.py:45
  92.4 0.0 reduce-scatter.14.cloned.1.call-start
  92.4 0.4 convolution_convert_fusion.3
  92.8 17.0 %all_gather.7 = bf16[1024,320]{1,0:T(8,128)(2,1)S(1)} all-gather(bf16[64,320]{1,0:T(8,128)(2,1)S(1)} %convolution_convert_fusion.3), channel_id=1, replica_groups=mesh['dp'=4,'tm'=16,'head'=4] {'tm'}, dimensions={0}, use_global_device_ids=true | all-gather | bytes 696320 | tf_op jit(solution)/shard_map/all_gather | solution.py:23
  109.8 0.3 copy.40
  110.1 4.1 fusion.20
  114.2 47.2 %psum.14 = f32[5,1024]{1,0:T(8,128)S(1)} all-reduce(f32[5,1024]{1,0:T(8,128)S(1)} %fusion.20), channel_id=1, replica_groups=mesh['dp'=4,'tm'=16,'head'=4] {'tm'}, use_global_device_ids=true, to_apply=%region_3.4 | all-reduce | flops 5120 | bytes 40960 | tf_op jit(solution)/shard_map/psum | solution.py:48
  161.4 42.5 %all-reduce.8.cloned.1.call-done = f32[5,1024,64]{1,2,0:T(8,128)} async-done(((f32[5,1024,64]{1,2,0:T(8,128)}), f32[5,1024,64]{1,2,0:T(8,128)}) %all-reduce.8.cloned.1.call-update) | async-done | bytes 1310736 | tf_op jit(solution)/shard_map/psum | solution.py:48
  203.9 2.5 fusion.5
  206.3 4.1 multiply_convert_fusion
  210.4 1.5 copy-done.2
  211.9 0.6 fusion.4
  212.5 1.2 copy.55
  213.7 0.0 reduce-scatter.14.cloned.1.call-update
  213.8 0.2 reduce-scatter.16.cloned.1.call-start
  214.0 4.3 fusion.7
  218.3 1.6 convolution_bitcast_fusion.1
  219.9 2.7 fusion.6
  222.6 1.6 convolution_bitcast_fusion.2
  224.2 47.0 %reduce-scatter.14.cloned.1.call-done = bf16[64,320]{1,0:T(8,128)(2,1)} async-done(((bf16[1024,320]{1,0:T(8,128)(2,1)}), bf16[64,320]{1,0:T(8,128)(2,1)}) %reduce-scatter.14.cloned.1.call-update) | async-done | bytes 40976
  271.1 1.1 convolution_convert_fusion
  272.2 0.9 copy.57
  273.1 0.0 all-reduce.10.cloned.1.call-start
  273.2 2.6 convolution_bitcast_fusion
  275.8 2.5 convolution_bitcast_fusion.3
  278.3 0.0 reduce-scatter.12.cloned.1.call-start
  278.3 0.6 fusion.21
  278.9 1.4 fusion.3
  280.4 0.6 dynamic-slice
  281.6 12.0 %reduce-scatter.16.cloned.1.call-done = bf16[320,64]{1,0:T(8,128)(2,1)} async-done(((bf16[1280,64]{1,0:T(8,128)(2,1)}), bf16[320,64]{1,0:T(8,128)(2,1)}) %reduce-scatter.16.cloned.1.call-update) | async-done | bytes 40976
  293.6 1.6 copy.58
  295.2 206.0 %all-reduce.10.cloned.1.call-done = (f32[1280,320]{0,1:T(8,128)}, f32[1280,320]{0,1:T(8,128)}, f32[1280,320]{0,1:T(8,128)}, f32[1280,320]{0,1:T(8,128)}) async-done(((f32[1280,320]{0,1:T(8,128)}, f32[1280,320]{0,1:T(8,128)}, f32[1280,320]{0,1:T(8,128)}, f32[1280,320]{0,1:T(8,128)}), (f32[1280,320]{0,1:T(8,128)}, f32[1280,320]{0,1:T(8,128)}, f32[1280,320]{0,1:T(8,128)}, ...) | async-done | bytes 6553616
  501.2 1.2 constant_dynamic-slice_fusion.1
  502.4 0.7 copy.46
  503.2 0.7 copy.47
  503.9 1.2 dynamic-slice_bitcast_fusion
  505.1 0.7 copy.48
  505.8 0.7 copy.49
  506.6 18.8 %reduce-scatter.12.cloned.1.call-done = bf16[256,320]{0,1:T(8,128)(2,1)} async-done(((bf16[256,1280]{0,1:T(8,128)(2,1)}), bf16[256,320]{0,1:T(8,128)(2,1)}) %reduce-scatter.12.cloned.1.call-update) | async-done | bytes 163856 | tf_op jit(solution)/shard_map/reduce_scatter | solution.py:80
  (23 shorter events, 0.1 us)
Async XLA Ops:
  7.2 1.2 copy-start
  7.2 196.7 %all-reduce.8.cloned.1.call-start = ((), (), s32[]{:S(2)}) async-start(), calls=%async_computation.3 | async-start | bytes 2621440 | tf_op jit(solution)/shard_map/psum | solution.py:48
  85.5 7.0 %copy-start.6 = (bf16[320,1280]{1,0:T(8,128)(2,1)S(1)}, bf16[320,1280]{1,0:T(8,128)(2,1)}, u32[]{:S(2)}) copy-start(bf16[320,1280]{1,0:T(8,128)(2,1)} %param.15) | copy-start | bytes 2457604
  85.5 7.0 %copy-start.8 = (bf16[1,64,1280]{2,1,0:T(8,128)(2,1)S(1)}, bf16[1,64,1280]{2,1,0:T(8,128)(2,1)}, u32[]{:S(2)}) copy-start(bf16[1,64,1280]{2,1,0:T(8,128)(2,1)} %param.9) | copy-start | bytes 491524
  92.4 178.8 %reduce-scatter.14.cloned.1.call-start = ((), (), s32[]{:S(2)}) async-start(), calls=%async_computation.5 | async-start | bytes 835584
  110.0 100.4 %copy-start.5 = (bf16[1024,320]{0,1:T(8,128)(2,1)}, bf16[1024,320]{0,1:T(8,128)(2,1)S(1)}, u32[]{:S(2)}) copy-start(bf16[1024,320]{0,1:T(8,128)(2,1)S(1)} %copy.40) | copy-start | bytes 1966084
  210.4 1.5 copy-start.2
  213.8 4.6 copy-start.1
  213.8 79.8 %reduce-scatter.16.cloned.1.call-start = ((), (), s32[]{:S(2)}) async-start(), calls=%async_computation.6 | async-start | bytes 409600
  218.3 52.8 %copy-start.4 = (bf16[1280,320]{0,1:T(8,128)(2,1)S(1)}, bf16[1280,320]{0,1:T(8,128)(2,1)}, u32[]{:S(2)}) copy-start(bf16[1280,320]{0,1:T(8,128)(2,1)} %param.12) | copy-start | bytes 2457604
  219.9 55.8 %copy-start.7 = (bf16[1,64,1280]{2,1,0:T(8,128)(2,1)S(1)}, bf16[1,64,1280]{2,1,0:T(8,128)(2,1)}, u32[]{:S(2)}) copy-start(bf16[1,64,1280]{2,1,0:T(8,128)(2,1)} %param.8) | copy-start | bytes 491524
  273.1 228.1 %all-reduce.10.cloned.1.call-start = ((), (), s32[]{:S(2)}) async-start(), calls=%async_computation.7 | async-start | bytes 13107200
  275.8 3.1 copy-start.3
  278.2 2.1 copy-start.9
  278.3 247.1 %reduce-scatter.12.cloned.1.call-start = ((), (), s32[]{:S(2)}) async-start(), calls=%async_computation.4 | async-start | bytes 819200 | tf_op jit(solution)/shard_map/reduce_scatter | solution.py:80
Sparse Core Ops, SparseCore 0:
  92.5 111.3 all-reduce.7
  213.9 57.2 reduce-scatter.13
  273.8 19.7 reduce-scatter.15
  298.0 203.1 all-reduce.9
  504.2 21.1 reduce-scatter.11
where the time goes:
time: 535 us; the launch traced here: 532 us
  waiting for transfers between devices  326 us (61%)
  blocking collectives  132 us (25%)
  matrix products  38.3 us (7%)
  between operations  15.3 us (3%)
  local copies, waits for them, and re-layouts  12.8 us (2%)
  other arithmetic  6.59 us (1%)
    unnamed x8, waiting for transfers between devices  265 us
    psum x1, blocking collectives, per_device(): row_sum, out_sum = lax.psum((local_sum, local_out), 'tm')  47.2 us
    pmax x1, blocking collectives, per_device(): row_top = lax.pmax(local_top, 'tm')  45.9 us
    psum x1, waiting for transfers between devices, per_device(): row_sum, out_sum = lax.psum((local_sum, local_out), 'tm')  42.5 us
    all_gather x1, blocking collectives, per_device(): lax.all_gather(query_part, 'tm', axis=0, tiled=True)  22.1 us
    reduce_scatter x1, waiting for transfers between devices, per_device(): lax.psum_scatter(frame_term.astype(jnp.bfloat16), 'head', scatter_dimensi...  18.8 us
    all_gather x1, blocking collectives, per_device(): lax.all_gather(dout_part, 'tm', axis=0, tiled=True)  17 us
    unnamed x29, local copies, waits for them, and re-layouts  11.1 us
  transfers between devices with their start and end apart: 5, of which 5 were waited for; matrix products, arithmetic and copies ran while one was open for 6% of the time, Pallas kernels for 0%

commit v1 on v0

v1 whole, which is shorter than its diff:
```python
import functools
import math

import jax
import jax.numpy as jnp
from jax import lax
from jax.experimental import pallas as pl
from jax.experimental.pallas import tpu as pltpu
from jax.sharding import Mesh, PartitionSpec as P

HD = 64
BF = jnp.bfloat16
F32 = jnp.float32
SCALE = HD ** (-0.5)
LOG2 = SCALE * math.log2(math.e)
LOW = -1e30
NT = (((1,), (1,)), ((), ()))
TN = (((0,), (0,)), ((), ()))


def mm(left, right, dims=None):
    if dims is None:
        dims = (((1,), (0,)), ((), ()))
    return lax.dot_general(left, right, dims, preferred_element_type=F32)


def ring(x, axis, size, step):
    return lax.ppermute(x, axis, [(i, (i + step) % size) for i in range(size)])


def swap(x, axis):
    return lax.ppermute(x, axis, [(0, 1), (1, 0)])


def frame_bias(valid_ref, block, rows):
    positions = lax.broadcasted_iota(jnp.int32, (rows, 1), 0)
    return jnp.where(positions < valid_ref[block], 0.0, LOW)


def stats_kernel(heads, valid_ref, *refs):
    rows_refs, frame_refs, out_ref = refs[:4], refs[4:8], refs[8]
    width = heads * HD
    rows = jnp.concatenate([r[...] for r in rows_refs], axis=0)
    blocks = [r[...] for r in frame_refs]
    biases = [frame_bias(valid_ref, j, b.shape[0]) for j, b in enumerate(blocks)]
    out_ref[...] = jnp.zeros_like(out_ref)
    for h in range(heads):
        cut = slice(h * HD, (h + 1) * HD)
        cut2 = slice(width + h * HD, width + (h + 1) * HD)
        query, dout = rows[:, cut], rows[:, cut2]
        scores = [
            mm(b[:, cut], query, NT) * LOG2 + bias for b, bias in zip(blocks, biases)
        ]
        top = functools.reduce(
            jnp.maximum, [jnp.max(s, axis=0, keepdims=True) for s in scores]
        )
        top = jnp.maximum(top, 0.1 * LOW)
        total = jnp.zeros_like(top)
        delta = jnp.zeros_like(top)
        for s, b in zip(scores, blocks):
            weight = jnp.exp2(s - top)
            dprobs = mm(b[:, cut2], dout, NT)
            total += jnp.sum(weight, axis=0, keepdims=True)
            delta += jnp.sum(weight * dprobs, axis=0, keepdims=True)
        total = jnp.maximum(total, 1.0)
        out_ref[h : h + 1, :] = top + jnp.log2(total)
        out_ref[8 + h : 9 + h, :] = delta / total


def grads_kernel(heads, valid_ref, *refs):
    rows_refs, frame_refs, stat_refs = refs[:4], refs[4:8], refs[8:12]
    keep_ref, send_ref = refs[12:14]
    dq_refs = refs[14:18]
    width = heads * HD
    rows = jnp.concatenate([r[...] for r in rows_refs], axis=0)
    blocks = [r[...] for r in frame_refs]
    part = blocks[0].shape[0]
    own = rows_refs[0].shape[0]
    stats = [stat_refs[0][...]] + [
        pltpu.roll(stat_refs[k][...], own * k, 1) for k in (1, 2, 3)
    ]
    tops = [s[:8] for s in stats]
    top = functools.reduce(jnp.maximum, tops)
    shares = [jnp.exp2(t - top) for t in tops]
    total = functools.reduce(jnp.add, shares)
    lse = top + jnp.log2(total)
    delta = functools.reduce(
        jnp.add, [w * s[8:] for w, s in zip(shares, stats)]
    ) / total
    biases = [frame_bias(valid_ref, j, part) for j in range(4)]
    dq_t, att_t = [], []
    for h in range(heads):
        cut = slice(h * HD, (h + 1) * HD)
        cut2 = slice(width + h * HD, width + (h + 1) * HD)
        query, dout = rows[:, cut], rows[:, cut2]
        dq_sum = jnp.zeros((HD, rows.shape[0]), F32)
        att_sum = jnp.zeros((HD, rows.shape[0]), F32)
        for j, (b, bias) in enumerate(zip(blocks, biases)):
            key, value = b[:, cut], b[:, cut2]
            scores = mm(key, query, NT) * LOG2 + bias
            probs = jnp.exp2(scores - lse[h : h + 1])
            dprobs = mm(value, dout, NT)
            dscores = (probs * (dprobs - delta[h : h + 1])).astype(BF)
            probs = probs.astype(BF)
            dkey = mm(dscores, query) * SCALE
            dvalue = mm(probs, dout)
            out_ref = send_ref if j % 2 else keep_ref
            span = slice((j // 2) * part, (j // 2 + 1) * part)
            out_ref[span, cut] = dkey.astype(out_ref.dtype)
            out_ref[span, cut2] = dvalue.astype(out_ref.dtype)
            dq_sum += mm(key, dscores, TN)
            att_sum += mm(value, probs, TN)
        dq_t.append(dq_sum * SCALE)
        att_t.append(att_sum)
    joined = jnp.concatenate(dq_t + att_t, axis=0).T
    for k in range(4):
        dq_refs[k][...] = joined[k * own : (k + 1) * own].astype(dq_refs[k].dtype)


def weights_kernel(part, xt_ref, xt2_ref, y_ref, y2_ref, *out_refs):
    frames = y_ref.shape[0] - part
    half = y_ref.shape[1] // 2
    step = out_refs[0].shape[0]
    pairs = ((xt_ref, y_ref), (xt2_ref, y2_ref))
    for k, out_ref in enumerate(out_refs):
        span = slice(k * step, (k + 1) * step)
        kv = sum(mm(x[span, :frames], y[:frames, :]) for x, y in pairs)
        q = sum(
            mm(x[span, frames : frames + part], y[frames : frames + part, :half])
            for x, y in pairs
        )
        o = sum(
            mm(x[span, frames + part :], y[frames : frames + part, half:])
            for x, y in pairs
        )
        out_ref[:, : 2 * half] = kv.astype(out_ref.dtype)
        out_ref[:, 2 * half : 3 * half] = q.astype(out_ref.dtype)
        out_ref[:, 3 * half :] = o.astype(out_ref.dtype)


VMEM = pl.BlockSpec(memory_space=pltpu.VMEM)
SMEM = pl.BlockSpec(memory_space=pltpu.SMEM)
PARAMS = pltpu.CompilerParams(vmem_limit_bytes=48 * 1024 * 1024)


def per_device(query_in, grad_out, encoder_states, frame_lengths, w_query, w_key, w_value, w_out):
    rows_in, rows_grad, frames = query_in[0], grad_out[0], encoder_states[0]
    width = w_query.shape[1]
    heads = width // HD
    model = w_query.shape[0]
    own, slab = rows_in.shape[0], frames.shape[0]
    xi, ai, bi, ci, yi = (lax.axis_index(n) for n in ("dp", "a", "b", "core", "head"))

    query = mm(rows_in, w_query).astype(BF)
    dout = mm(rows_grad, w_out, NT).astype(BF)
    rows0 = jnp.concatenate([query, dout], axis=1)
    row_blocks = [rows0] + [ring(rows0, "a", 4, j) for j in (1, 2, 3)]

    w_kv = jnp.concatenate([w_key, w_value], axis=1)
    kv = mm(frames, w_kv).astype(BF)
    kv_pair = swap(kv, "b")
    frame_blocks = [kv, swap(kv, "core"), kv_pair, swap(kv_pair, "core")]
    starts = [
        slab * (4 * ai + 2 * (bi ^ db) + (ci ^ dc)) for db in (0, 1) for dc in (0, 1)
    ]
    valid = jnp.stack([frame_lengths[0] - s for s in starts]).astype(jnp.int32)

    place = jnp.arange(model, dtype=jnp.int32)
    inner = model // 64
    rest, unit = place // inner, place % inner
    a_rel, b_rel = rest % 4, (rest // 4) % 2
    x_rel, c_rel = (rest // 8) % 4, rest // 32
    target = (
        ((x_rel + xi) % 4) * 16 + ((a_rel + ai) % 4) * 4 + (b_rel ^ bi) * 2 + (c_rel ^ ci)
    ) * inner + unit
    pick = (place[:, None] == target[None, :]).astype(BF)
    stacked = jnp.concatenate([frames, rows_in, rows_grad], axis=0)
    turned = mm(pick, stacked, (((0,), (1,)), ((), ()))).astype(BF)
    turned_own = turned[: model // 2]
    turned_other = swap(turned[model // 2 :], "core")

    stats = pl.pallas_call(
        functools.partial(stats_kernel, heads),
        out_shape=jax.ShapeDtypeStruct((16, 4 * own), F32),
        in_specs=[SMEM] + [VMEM] * 8,
        out_specs=VMEM,
        compiler_params=PARAMS,
    )(valid, *row_blocks, *frame_blocks)
    all_stats = [stats] + [ring(stats, "a", 4, j) for j in (1, 2, 3)]

    keep, send, dq0, dq1, dq2, dq3 = pl.pallas_call(
        functools.partial(grads_kernel, heads),
        out_shape=[
            jax.ShapeDtypeStruct((2 * slab, 2 * width), F32),
            jax.ShapeDtypeStruct((2 * slab, 2 * width), BF),
            jax.ShapeDtypeStruct((own, 2 * width), F32),
        ]
        + [jax.ShapeDtypeStruct((own, 2 * width), BF)] * 3,
        in_specs=[SMEM] + [VMEM] * 12,
        out_specs=[VMEM] * 6,
        compiler_params=PARAMS,
    )(valid, *row_blocks, *frame_blocks, *all_stats)

    recv = swap(send, "core").astype(F32)
    pair = (keep[slab:] + recv[slab:]).astype(BF)
    pair_recv = swap(pair, "b").astype(F32)
    dq_recv = [ring(d, "a", 4, -j).astype(F32) for j, d in ((1, dq1), (2, dq2), (3, dq3))]
    dkv = (keep[:slab] + recv[:slab] + pair_recv).astype(BF)
    dqo = (dq0 + dq_recv[0] + dq_recv[1] + dq_recv[2]).astype(BF)
    grads = jnp.concatenate([dkv, dqo], axis=0)
    grads_other = swap(grads, "core")

    parts = []
    for k in range(4):
        start = ((yi + k) % 4) * width
        w_kv_rows = lax.dynamic_slice_in_dim(w_kv, start, width, 0)
        w_q_rows = lax.dynamic_slice_in_dim(w_query, start, width, 0)
        parts.append(
            jnp.concatenate(
                [mm(dkv, w_kv_rows, NT), mm(dqo[:, :width], w_q_rows, NT)], axis=0
            ).astype(BF if k else F32)
        )
    arrived = [ring(parts[k], "head", 4, k).astype(F32) for k in (1, 2, 3)]
    inputs = (parts[0] + arrived[0] + arrived[1] + arrived[2]).astype(BF)
    dframes, dinput = inputs[:slab], inputs[slab:]

    step = model // 8
    pieces = pl.pallas_call(
        functools.partial(weights_kernel, own),
        out_shape=[jax.ShapeDtypeStruct((step, 4 * width), F32)]
        + [jax.ShapeDtypeStruct((step, 4 * width), BF)] * 3,
        in_specs=[VMEM] * 4,
        out_specs=[VMEM] * 4,
        compiler_params=PARAMS,
    )(turned_own, turned_other, grads, grads_other)
    over_x = [ring(pieces[k], "dp", 4, k).astype(F32) for k in (1, 2, 3)]
    total = pieces[0] + over_x[0] + over_x[1] + over_x[2]
    total = total[: step // 2] + swap(total[step // 2 :].astype(BF), "b").astype(F32)
    low = total.astype(BF)
    over_a = [
        ring(low[k * inner : (k + 1) * inner], "a", 4, k).astype(F32) for k in (1, 2, 3)
    ]
    total = total[:inner] + over_a[0] + over_a[1] + over_a[2]
    return (
        dinput[None],
        dframes[None],
        total[:, 2 * width : 3 * width],
        total[:, :width],
        total[:, width : 2 * width],
        total[:, 3 * width :].T,
    )


def solution(mesh):
    dp, tm, head = mesh.devices.shape
    fine = Mesh(mesh.devices.reshape(dp, 4, 2, 2, head), ("dp", "a", "b", "core", "head"))
    tm = ("a", "b", "core")
    placed = (
        P("dp", tm, None),
        P("dp", tm, None),
        P("dp", tm, None),
        P("dp"),
        P(None, "head"),
        P(None, "head"),
        P(None, "head"),
        P("head", None),
    )
    every = ("dp",) + tm
    return jax.shard_map(
        per_device,
        mesh=fine,
        in_specs=placed,
        out_specs=(
            P("dp", tm, "head"),
            P("dp", tm, "head"),
            P(every, "head"),
            P(every, "head"),
            P(every, "head"),
            P("head", every),
        ),
        check_vma=False,
    )
```

time: 535 us -> 132 us (0.25)
  waiting for transfers between devices: 326 us -> 48.2 us
  blocking collectives: 132 us -> 0 us
  starting transfers between devices: 0.39 us -> 46.6 us
  matrix products: 38.3 us -> 8.95 us
  between operations: 15.3 us -> 1.72 us
  Pallas kernels: 0 us -> 10.7 us
    unnamed x8 -> x0, waiting for transfers between devices: 265 us -> none
    ppermute x0 -> x26, waiting for transfers between devices: none -> 48.2 us  [the longest x18 34.2 us: ring(): return lax.ppermute(x, axis, [(i, (i + step) % size) for i in range(size)])]
    psum x1 -> x0, blocking collectives: 47.2 us -> none  [per_device(): row_sum, out_sum = lax.psum((local_sum, local_out), 'tm')]
    ppermute x0 -> x26, starting transfers between devices: none -> 46.6 us  [the longest x18 42.7 us: ring(): return lax.ppermute(x, axis, [(i, (i + step) % size) for i in range(size)])]
    pmax x1 -> x0, blocking collectives: 45.9 us -> none  [per_device(): row_top = lax.pmax(local_top, 'tm')]
    psum x1 -> x0, waiting for transfers between devices: 42.5 us -> none  [per_device(): row_sum, out_sum = lax.psum((local_sum, local_out), 'tm')]
    all_gather x2 -> x0, blocking collectives: 39.1 us -> none  [the longest x1 22.1 us: per_device(): lax.all_gather(query_part, 'tm', axis=0, tiled=True)]
    dot_general x17 -> x12, matrix products: 38.3 us -> 8.95 us  [mm(): return lax.dot_general(left, right, dims, preferred_element_type=F32)]
  transfers between devices with their start and end apart: 5 -> 26, of which waited for: 5 -> 15; matrix products, arithmetic and copies ran while one was open for 6% -> 14% of each run, Pallas kernels for 0% -> 1%
where the time goes in v1:
time: 132 us
  waiting for transfers between devices  48.2 us (37%)
  starting transfers between devices  46.6 us (35%)
  local copies, waits for them, and re-layouts  12.3 us (9%)
  Pallas kernels  10.7 us (8%)
  matrix products  8.95 us (7%)
  other arithmetic  3.04 us (2%)
  between operations  1.72 us (1%)
    ppermute x18, starting transfers between devices, ring(): return lax.ppermute(x, axis, [(i, (i + step) % size) for i in range(size)])  42.7 us
    ppermute x18, waiting for transfers between devices, ring(): return lax.ppermute(x, axis, [(i, (i + step) % size) for i in range(size)])  34.2 us
    ppermute x8, waiting for transfers between devices, swap(): return lax.ppermute(x, axis, [(0, 1), (1, 0)])  14 us
    dot_general x12, matrix products, mm(): return lax.dot_general(left, right, dims, preferred_element_type=F32)  8.95 us
    pallas_call x1, Pallas kernels, per_device(): pl.pallas_call(functools.partial(grads_kernel, heads), out_shape=[jax.Sha...  6.94 us
    unnamed x38, local copies, waits for them, and re-layouts  5.29 us
    another operation x3, local copies, waits for them, and re-layouts  4.6 us
    ppermute x8, starting transfers between devices, swap(): return lax.ppermute(x, axis, [(0, 1), (1, 0)])  3.87 us
  transfers between devices with their start and end apart: 26, of which 15 were waited for; matrix products, arithmetic and copies ran while one was open for 14% of the time, Pallas kernels for 1%

profile of v1, /device:TPU:8, one launch (start us, length us, event | category | flops | bytes accessed | tf_op | source)
XLA Modules:
  0.0 131.5 jit_solution(13217367124871056171)
XLA Ops:
  0.7 1.3 %constant_dynamic-update-slice_fusion.1 = bf16[1280,640]{0,1:T(8,128)(2,1)S(1)} fusion(bf16[1280,320]{0,1:T(8,128)(2,1)} %param.13), kind=kLoop, calls=%fused_computation.115 | loop fusion | bytes 1638400
  3.1 2.0 %collective-permute-start.4 = (bf16[256,640]{1,0:T(8,128)(2,1)S(1)}, bf16[256,640]{1,0:T(8,128)(2,1)S(1)}, u32[]{:S(2)}, u32[]{:S(2)}) collective-permute-start(bf16[256,640]{1,0:T(8,128)(2,1)S(1)} %fusion.7.refs_4_), channel_id=1, source_target_pairs={{0,8},{8,0},{1,9},{9,1},{2,10},{10,2},{3,11},{11,3},{4,12},{12,4},... | collective-permute-start | bytes 983048 | tf_op jit(solution)/shard_map/ppermute | solution.py:32
  5.9 7.5 %collective-permute-done.4.refs_6_ = bf16[256,640]{1,0:T(8,128)(2,1)S(1)} collective-permute-done((bf16[256,640]{1,0:T(8,128)(2,1)S(1)}, bf16[256,640]{1,0:T(8,128)(2,1)S(1)}, u32[]{:S(2)}, u32[]{:S(2)}) %collective-permute-start.4) | collective-permute-done | bytes 327712 | tf_op jit(solution)/shard_map/ppermute | solution.py:32
  13.5 3.3 %collective-permute-start = (bf16[64,640]{1,0:T(8,128)(2,1)S(1)}, bf16[64,640]{1,0:T(8,128)(2,1)S(1)}, u32[]{:S(2)}, u32[]{:S(2)}) collective-permute-start(bf16[64,640]{1,0:T(8,128)(2,1)S(1)} %pad_maximum_fusion.4.refs_0_), channel_id=1, source_target_pairs={{0,16},{16,32},{32,48},{48,0},{1,17},{17,33},{33,49},{49,1},{2,18}... | collective-permute-start | bytes 245768 | tf_op jit(solution)/shard_map/ppermute | solution.py:28
  16.9 5.2 %collective-permute-start.1 = (bf16[64,640]{1,0:T(8,128)(2,1)S(1)}, bf16[64,640]{1,0:T(8,128)(2,1)S(1)}, u32[]{:S(2)}, u32[]{:S(2)}) collective-permute-start(bf16[64,640]{1,0:T(8,128)(2,1)S(1)} %pad_maximum_fusion.4.refs_0_), channel_id=1, source_target_pairs={{0,32},{16,48},{32,0},{48,16},{1,33},{17,49},{33,1},{49,17},{2,34}... | collective-permute-start | bytes 245768 | tf_op jit(solution)/shard_map/ppermute | solution.py:28
  22.1 2.7 %collective-permute-start.2 = (bf16[64,640]{1,0:T(8,128)(2,1)S(1)}, bf16[64,640]{1,0:T(8,128)(2,1)S(1)}, u32[]{:S(2)}, u32[]{:S(2)}) collective-permute-start(bf16[64,640]{1,0:T(8,128)(2,1)S(1)} %pad_maximum_fusion.4.refs_0_), channel_id=1, source_target_pairs={{0,48},{16,0},{32,16},{48,32},{1,49},{17,1},{33,17},{49,33},{2,50}... | collective-permute-start | bytes 245768 | tf_op jit(solution)/shard_map/ppermute | solution.py:28
  25.6 2.9 %collective-permute-done.1.refs_2_ = bf16[64,640]{1,0:T(8,128)(2,1)S(1)} collective-permute-done((bf16[64,640]{1,0:T(8,128)(2,1)S(1)}, bf16[64,640]{1,0:T(8,128)(2,1)S(1)}, u32[]{:S(2)}, u32[]{:S(2)}) %collective-permute-start.1) | collective-permute-done | bytes 81952 | tf_op jit(solution)/shard_map/ppermute | solution.py:28
  28.5 2.3 %collective-permute-done.2.refs_3_ = bf16[64,640]{1,0:T(8,128)(2,1)S(1)} collective-permute-done((bf16[64,640]{1,0:T(8,128)(2,1)S(1)}, bf16[64,640]{1,0:T(8,128)(2,1)S(1)}, u32[]{:S(2)}, u32[]{:S(2)}) %collective-permute-start.2) | collective-permute-done | bytes 81952 | tf_op jit(solution)/shard_map/ppermute | solution.py:28
  30.8 2.5 %shard_map.127.refs_8_ = f32[16,256]{1,0:T(8,128)S(1)} custom-call(s32[4]{0:T(128)S(1)} %pad_add_fusion.valid_ref, bf16[64,640]{1,0:T(8,128)(2,1)S(1)} %pad_maximum_fusion.4.refs_0_, bf16[64,640]{1,0:T(8,128)(2,1)S(1)} %collective-permute-done.refs_1_, bf16[64,640]{1,0:T(8,128)(2,1)S(1)} %collective-permute-done.1.refs_2_, ...), custom_call_target="tpu_custom_call" | custom-call | tf_op jit(solution)/shard_map/pallas_call | solution.py:182
  33.3 1.4 %collective-permute-start.6 = (f32[16,256]{1,0:T(8,128)S(1)}, f32[16,256]{1,0:T(8,128)S(1)}, u32[]{:S(2)}, u32[]{:S(2)}) collective-permute-start(f32[16,256]{1,0:T(8,128)S(1)} %shard_map.127.refs_8_), channel_id=1, source_target_pairs={{0,16},{16,32},{32,48},{48,0},{1,17},{17,33},{33,49},{49,1},{2,18}... | collective-permute-start | bytes 49160 | tf_op jit(solution)/shard_map/ppermute | solution.py:28
  34.7 4.6 %collective-permute-start.7 = (f32[16,256]{1,0:T(8,128)S(1)}, f32[16,256]{1,0:T(8,128)S(1)}, u32[]{:S(2)}, u32[]{:S(2)}) collective-permute-start(f32[16,256]{1,0:T(8,128)S(1)} %shard_map.127.refs_8_), channel_id=1, source_target_pairs={{0,32},{16,48},{32,0},{48,16},{1,33},{17,49},{33,1},{49,17},{2,34}... | collective-permute-start | bytes 49160 | tf_op jit(solution)/shard_map/ppermute | solution.py:28
  39.3 2.4 %collective-permute-start.8 = (f32[16,256]{1,0:T(8,128)S(1)}, f32[16,256]{1,0:T(8,128)S(1)}, u32[]{:S(2)}, u32[]{:S(2)}) collective-permute-start(f32[16,256]{1,0:T(8,128)S(1)} %shard_map.127.refs_8_), channel_id=1, source_target_pairs={{0,48},{16,0},{32,16},{48,32},{1,49},{17,1},{33,17},{49,33},{2,50}... | collective-permute-start | bytes 49160 | tf_op jit(solution)/shard_map/ppermute | solution.py:28
  41.7 1.9 %fusion.4 = bf16[1280,384]{1,0:T(8,128)(2,1)S(1)} fusion(s32[1280]{0:T(1024)S(1)} %fusion.50, bf16[64,1280]{1,0:T(8,128)(2,1)S(1)} %bitcast.33, bf16[64,1280]{1,0:T(8,128)(2,1)S(1)} %bitcast.34, bf16[256,1280]{1,0:T(8,128)(2,1)S(1)} %bitcast.35), kind=kOutput, calls=%fused_computation.4 | convolution fusion | flops 1265008640 | bytes 1971200 | tf_op jit(solution)/shard_map/dot_general | solution.py:24
  44.1 1.0 copy-done.2
  45.1 0.9 copy-done.4
  45.9 6.9 %shard_map.128 = (f32[512,640]{1,0:T(8,128)S(1)}, bf16[512,640]{1,0:T(8,128)(2,1)S(1)}, f32[64,640]{1,0:T(8,128)S(1)}, bf16[64,640]{1,0:T(8,128)(2,1)S(1)}, bf16...) custom-call(s32[4]{0:T(128)S(1)} %pad_add_fusion.valid_ref, bf16[64,640]{1,0:T(8,128)(2,1)S(1)} %pad_maximum_fusion.4.refs_0_, ...), custom_call_target="tpu_custom_call" | custom-call | tf_op jit(solution)/shard_map/pallas_call | solution.py:191
  52.9 1.7 %collective-permute-start.13 = (bf16[64,640]{1,0:T(8,128)(2,1)}, bf16[64,640]{1,0:T(8,128)(2,1)S(1)}, u32[]{:S(2)}, u32[]{:S(2)}) collective-permute-start(bf16[64,640]{1,0:T(8,128)(2,1)} %get-tuple-element.21), channel_id=1, source_target_pairs={{0,16},{16,32},{32,48},{48,0},{1,17},{17,33},{33,49},{49,1},{2,18}... | collective-permute-start | bytes 245768 | tf_op jit(solution)/shard_map/ppermute | solution.py:28
  54.6 4.1 %collective-permute-start.12 = (bf16[64,640]{1,0:T(8,128)(2,1)S(1)}, bf16[64,640]{1,0:T(8,128)(2,1)S(1)}, u32[]{:S(2)}, u32[]{:S(2)}) collective-permute-start(bf16[64,640]{1,0:T(8,128)(2,1)S(1)} %get-tuple-element.20), channel_id=1, source_target_pairs={{0,32},{16,48},{32,0},{48,16},{1,33},{17,49},{33,1},{49,17},{2,34}... | collective-permute-start | bytes 245768 | tf_op jit(solution)/shard_map/ppermute | solution.py:28
  58.7 1.1 collective-permute-start.11
  59.9 0.9 fusion.76
  61.3 1.5 %collective-permute-done.13 = bf16[64,640]{1,0:T(8,128)(2,1)S(1)} collective-permute-done((bf16[64,640]{1,0:T(8,128)(2,1)}, bf16[64,640]{1,0:T(8,128)(2,1)S(1)}, u32[]{:S(2)}, u32[]{:S(2)}) %collective-permute-start.13) | collective-permute-done | bytes 81952 | tf_op jit(solution)/shard_map/ppermute | solution.py:28
  62.7 0.8 collective-permute-done.12
  63.6 1.7 %collective-permute-done.11 = bf16[64,640]{1,0:T(8,128)(2,1)S(1)} collective-permute-done((bf16[64,640]{1,0:T(8,128)(2,1)S(1)}, bf16[64,640]{1,0:T(8,128)(2,1)S(1)}, u32[]{:S(2)}, u32[]{:S(2)}) %collective-permute-start.11) | collective-permute-done | bytes 81952 | tf_op jit(solution)/shard_map/ppermute | solution.py:28
  65.2 1.0 add_convert_fusion
  66.2 0.9 convolution_convert_fusion.4
  67.1 0.9 convolution_convert_fusion.5
  68.1 1.1 copy-done.7
  69.6 0.9 convolution_convert_fusion.6
  70.5 1.5 %copy.24 = bf16[64,320]{0,1:T(8,128)(2,1)} copy(bf16[64,320]{1,0:T(8,128)(2,1)} %convolution_convert_fusion.4) | data formatting | bytes 81920 | tf_op jit(solution)/shard_map/convert.2
  72.0 1.5 %copy.23 = bf16[64,320]{0,1:T(8,128)(2,1)} copy(bf16[64,320]{1,0:T(8,128)(2,1)} %convolution_convert_fusion.5) | data formatting | bytes 81920 | tf_op jit(solution)/shard_map/convert.4
  73.5 1.5 %copy.22 = bf16[64,320]{0,1:T(8,128)(2,1)} copy(bf16[64,320]{1,0:T(8,128)(2,1)} %convolution_convert_fusion.6) | data formatting | bytes 81920 | tf_op jit(solution)/shard_map/convert.6
  75.6 1.1 collective-permute-done.10
  76.7 1.3 fusion.15
  80.5 2.7 %collective-permute-start.15 = (bf16[320,320]{0,1:T(8,128)(2,1)S(1)}, bf16[320,320]{0,1:T(8,128)(2,1)S(1)}, u32[]{:S(2)}, u32[]{:S(2)}) collective-permute-start(bf16[320,320]{0,1:T(8,128)(2,1)S(1)} %pad_maximum_fusion.2), channel_id=1, source_target_pairs={{0,2},{1,3},{2,0},{3,1},{4,6},{5,7},{6,4},{7,5},{8,10},{9,11},{10,... | collective-permute-start | bytes 614408 | tf_op jit(solution)/shard_map/ppermute | solution.py:28
  83.3 2.0 %collective-permute-start.14 = (bf16[320,320]{0,1:T(8,128)(2,1)S(1)}, bf16[320,320]{0,1:T(8,128)(2,1)S(1)}, u32[]{:S(2)}, u32[]{:S(2)}) collective-permute-start(bf16[320,320]{0,1:T(8,128)(2,1)S(1)} %pad_maximum_fusion.1), channel_id=1, source_target_pairs={{0,1},{1,2},{2,3},{3,0},{4,5},{5,6},{6,7},{7,4},{8,9},{9,10},{10,1... | collective-permute-start | bytes 614408 | tf_op jit(solution)/shard_map/ppermute | solution.py:28
  85.3 1.3 shard_map.129
  86.6 2.7 %collective-permute-start.21 = (bf16[160,1280]{1,0:T(8,128)(2,1)S(1)}, bf16[160,1280]{1,0:T(8,128)(2,1)S(1)}, u32[]{:S(2)}, u32[]{:S(2)}) collective-permute-start(bf16[160,1280]{1,0:T(8,128)(2,1)S(1)} %get-tuple-element.25), channel_id=1, source_target_pairs={{0,192},{64,0},{128,64},{192,128},{1,193},{65,1},{129,65},{193,129... | collective-permute-start | bytes 1228808 | tf_op jit(solution)/shard_map/ppermute | solution.py:28
  89.3 0.8 collective-permute-start.20
  90.1 0.9 collective-permute-start.19
  92.0 3.9 %collective-permute-done.14 = bf16[320,320]{0,1:T(8,128)(2,1)S(1)} collective-permute-done((bf16[320,320]{0,1:T(8,128)(2,1)S(1)}, bf16[320,320]{0,1:T(8,128)(2,1)S(1)}, u32[]{:S(2)}, u32[]{:S(2)}) %collective-permute-start.14) | collective-permute-done | bytes 204832 | tf_op jit(solution)/shard_map/ppermute | solution.py:28
  96.0 11.0 %collective-permute-done.21 = bf16[160,1280]{1,0:T(8,128)(2,1)S(1)} collective-permute-done((bf16[160,1280]{1,0:T(8,128)(2,1)S(1)}, bf16[160,1280]{1,0:T(8,128)(2,1)S(1)}, u32[]{:S(2)}, u32[]{:S(2)}) %collective-permute-start.21) | collective-permute-done | bytes 409632 | tf_op jit(solution)/shard_map/ppermute | solution.py:28
  107.0 3.7 %collective-permute-done.19 = bf16[160,1280]{1,0:T(8,128)(2,1)S(1)} collective-permute-done((bf16[160,1280]{1,0:T(8,128)(2,1)S(1)}, bf16[160,1280]{1,0:T(8,128)(2,1)S(1)}, u32[]{:S(2)}, u32[]{:S(2)}) %collective-permute-start.19) | collective-permute-done | bytes 409632 | tf_op jit(solution)/shard_map/ppermute | solution.py:28
  110.8 1.0 collective-permute-start.22
  112.5 5.4 %collective-permute-done.22 = bf16[80,1280]{1,0:T(8,128)(2,1)S(1)} collective-permute-done((bf16[80,1280]{1,0:T(8,128)(2,1)S(1)}, bf16[80,1280]{1,0:T(8,128)(2,1)S(1)}, u32[]{:S(2)}, u32[]{:S(2)}) %collective-permute-start.22) | collective-permute-done | bytes 204832 | tf_op jit(solution)/shard_map/ppermute | solution.py:32
  118.0 2.9 %collective-permute-start.25 = (bf16[20,1280]{1,0:T(8,128)(2,1)S(1)}, bf16[20,1280]{1,0:T(8,128)(2,1)S(1)}, u32[]{:S(2)}, u32[]{:S(2)}) collective-permute-start(bf16[20,1280]{1,0:T(8,128)(2,1)S(1)} %get-tuple-element.43), channel_id=1, source_target_pairs={{0,48},{16,0},{32,16},{48,32},{1,49},{17,1},{33,17},{49,33},{2,50}... | collective-permute-start | bytes 153608 | tf_op jit(solution)/shard_map/ppermute | solution.py:28
  121.0 3.3 %collective-permute-start.24 = (bf16[20,1280]{1,0:T(8,128)(2,1)S(1)}, bf16[20,1280]{1,0:T(8,128)(2,1)S(1)}, u32[]{:S(2)}, u32[]{:S(2)}) collective-permute-start(bf16[20,1280]{1,0:T(8,128)(2,1)S(1)} %get-tuple-element.44), channel_id=1, source_target_pairs={{0,32},{16,48},{32,0},{48,16},{1,33},{17,49},{33,1},{49,17},{2,34}... | collective-permute-start | bytes 153608 | tf_op jit(solution)/shard_map/ppermute | solution.py:28
  125.0 5.1 %collective-permute-done.24 = bf16[20,1280]{1,0:T(8,128)(2,1)S(1)} collective-permute-done((bf16[20,1280]{1,0:T(8,128)(2,1)S(1)}, bf16[20,1280]{1,0:T(8,128)(2,1)S(1)}, u32[]{:S(2)}, u32[]{:S(2)}) %collective-permute-start.24) | collective-permute-done | bytes 51232 | tf_op jit(solution)/shard_map/ppermute | solution.py:28
  130.8 0.7 slice_bitcast_fusion.2
  (82 shorter events, 9.8 us)
Async XLA Ops:
  0.6 4.9 %copy-start = (bf16[1280,320]{0,1:T(8,128)(2,1)S(1)}, bf16[1280,320]{0,1:T(8,128)(2,1)}, u32[]{:S(2)}) copy-start(bf16[1280,320]{0,1:T(8,128)(2,1)} %param.12) | copy-start | bytes 2457604
  0.6 1.5 %copy-start.10 = (bf16[1280,320]{0,1:T(8,128)(2,1)S(1)}, bf16[1280,320]{0,1:T(8,128)(2,1)}, u32[]{:S(2)}) copy-start(bf16[1280,320]{0,1:T(8,128)(2,1)} %param.14) | copy-start | bytes 2457604
  0.7 1.6 %copy-start.17 = (bf16[1,256,1280]{2,1,0:T(8,128)(2,1)S(1)}, bf16[1,256,1280]{2,1,0:T(8,128)(2,1)}, u32[]{:S(2)}) copy-start(bf16[1,256,1280]{2,1,0:T(8,128)(2,1)} %param.10) | copy-start | bytes 1966084
  2.3 3.2 %copy-start.8 = (bf16[1280,640]{0,1:T(8,128)(2,1)}, bf16[1280,640]{0,1:T(8,128)(2,1)S(1)}, u32[]{:S(2)}) copy-start(bf16[1280,640]{0,1:T(8,128)(2,1)S(1)} %constant_dynamic-update-slice_fusion) | copy-start | bytes 4915204
  2.3 2.8 %copy-start.11 = (bf16[320,1280]{1,0:T(8,128)(2,1)S(1)}, bf16[320,1280]{1,0:T(8,128)(2,1)}, u32[]{:S(2)}) copy-start(bf16[320,1280]{1,0:T(8,128)(2,1)} %param.15) | copy-start | bytes 2457604
  2.3 2.8 %copy-start.15 = (bf16[1,64,1280]{2,1,0:T(8,128)(2,1)S(1)}, bf16[1,64,1280]{2,1,0:T(8,128)(2,1)}, u32[]{:S(2)}) copy-start(bf16[1,64,1280]{2,1,0:T(8,128)(2,1)} %param.9) | copy-start | bytes 491524
  2.3 3.2 %copy-start.16 = (bf16[1,64,1280]{2,1,0:T(8,128)(2,1)S(1)}, bf16[1,64,1280]{2,1,0:T(8,128)(2,1)}, u32[]{:S(2)}) copy-start(bf16[1,64,1280]{2,1,0:T(8,128)(2,1)} %param.8) | copy-start | bytes 491524
  3.0 27.7 %collective-permute-start.3 = (bf16[256,640]{1,0:T(8,128)(2,1)S(1)}, bf16[256,640]{1,0:T(8,128)(2,1)S(1)}, u32[]{:S(2)}, u32[]{:S(2)}) collective-permute-start(bf16[256,640]{1,0:T(8,128)(2,1)S(1)} %fusion.7.refs_4_), channel_id=1, source_target_pairs={{0,4},{4,0},{1,5},{5,1},{2,6},{6,2},{3,7},{7,3},{8,12},{12,8},{9,1... | collective-permute-start | bytes 983048 | tf_op jit(solution)/shard_map/ppermute | solution.py:32
  3.1 10.3 %collective-permute-start.4 = (bf16[256,640]{1,0:T(8,128)(2,1)S(1)}, bf16[256,640]{1,0:T(8,128)(2,1)S(1)}, u32[]{:S(2)}, u32[]{:S(2)}) collective-permute-start(bf16[256,640]{1,0:T(8,128)(2,1)S(1)} %fusion.7.refs_4_), channel_id=1, source_target_pairs={{0,8},{8,0},{1,9},{9,1},{2,10},{10,2},{3,11},{11,3},{4,12},{12,4},... | collective-permute-start | bytes 983048 | tf_op jit(solution)/shard_map/ppermute | solution.py:32
  13.4 17.3 %collective-permute-start.5 = (bf16[256,640]{1,0:T(8,128)(2,1)S(1)}, bf16[256,640]{1,0:T(8,128)(2,1)S(1)}, u32[]{:S(2)}, u32[]{:S(2)}) collective-permute-start(bf16[256,640]{1,0:T(8,128)(2,1)S(1)} %collective-permute-done.4.refs_6_), channel_id=1, source_target_pairs={{0,4},{4,0},{1,5},{5,1},{2,6},{6,2},{3,7},{7,3},{8,12},{12,8},{9,1... | collective-permute-start | bytes 983048 | tf_op jit(solution)/shard_map/ppermute | solution.py:32
  13.5 12.0 %collective-permute-start = (bf16[64,640]{1,0:T(8,128)(2,1)S(1)}, bf16[64,640]{1,0:T(8,128)(2,1)S(1)}, u32[]{:S(2)}, u32[]{:S(2)}) collective-permute-start(bf16[64,640]{1,0:T(8,128)(2,1)S(1)} %pad_maximum_fusion.4.refs_0_), channel_id=1, source_target_pairs={{0,16},{16,32},{32,48},{48,0},{1,17},{17,33},{33,49},{49,1},{2,18}... | collective-permute-start | bytes 245768 | tf_op jit(solution)/shard_map/ppermute | solution.py:28
  16.9 11.6 %collective-permute-start.1 = (bf16[64,640]{1,0:T(8,128)(2,1)S(1)}, bf16[64,640]{1,0:T(8,128)(2,1)S(1)}, u32[]{:S(2)}, u32[]{:S(2)}) collective-permute-start(bf16[64,640]{1,0:T(8,128)(2,1)S(1)} %pad_maximum_fusion.4.refs_0_), channel_id=1, source_target_pairs={{0,32},{16,48},{32,0},{48,16},{1,33},{17,49},{33,1},{49,17},{2,34}... | collective-permute-start | bytes 245768 | tf_op jit(solution)/shard_map/ppermute | solution.py:28
  22.1 8.6 %collective-permute-start.2 = (bf16[64,640]{1,0:T(8,128)(2,1)S(1)}, bf16[64,640]{1,0:T(8,128)(2,1)S(1)}, u32[]{:S(2)}, u32[]{:S(2)}) collective-permute-start(bf16[64,640]{1,0:T(8,128)(2,1)S(1)} %pad_maximum_fusion.4.refs_0_), channel_id=1, source_target_pairs={{0,48},{16,0},{32,16},{48,32},{1,49},{17,1},{33,17},{49,33},{2,50}... | collective-permute-start | bytes 245768 | tf_op jit(solution)/shard_map/ppermute | solution.py:28
  30.7 12.9 %copy-start.3 = (bf16[64,640]{1,0:T(8,128)(2,1)}, bf16[64,640]{1,0:T(8,128)(2,1)S(1)}, u32[]{:S(2)}) copy-start(bf16[64,640]{1,0:T(8,128)(2,1)S(1)} %collective-permute-done.2.refs_3_) | copy-start | bytes 245764
  30.7 12.9 %copy-start.1 = (bf16[256,640]{1,0:T(8,128)(2,1)}, bf16[256,640]{1,0:T(8,128)(2,1)S(1)}, u32[]{:S(2)}) copy-start(bf16[256,640]{1,0:T(8,128)(2,1)S(1)} %collective-permute-done.5.refs_7_) | copy-start | bytes 983044
  33.3 10.4 %collective-permute-start.6 = (f32[16,256]{1,0:T(8,128)S(1)}, f32[16,256]{1,0:T(8,128)S(1)}, u32[]{:S(2)}, u32[]{:S(2)}) collective-permute-start(f32[16,256]{1,0:T(8,128)S(1)} %shard_map.127.refs_8_), channel_id=1, source_target_pairs={{0,16},{16,32},{32,48},{48,0},{1,17},{17,33},{33,49},{49,1},{2,18}... | collective-permute-start | bytes 49160 | tf_op jit(solution)/shard_map/ppermute | solution.py:28
  34.7 9.0 %collective-permute-start.7 = (f32[16,256]{1,0:T(8,128)S(1)}, f32[16,256]{1,0:T(8,128)S(1)}, u32[]{:S(2)}, u32[]{:S(2)}) collective-permute-start(f32[16,256]{1,0:T(8,128)S(1)} %shard_map.127.refs_8_), channel_id=1, source_target_pairs={{0,32},{16,48},{32,0},{48,16},{1,33},{17,49},{33,1},{49,17},{2,34}... | collective-permute-start | bytes 49160 | tf_op jit(solution)/shard_map/ppermute | solution.py:28
  39.3 4.8 %collective-permute-start.8 = (f32[16,256]{1,0:T(8,128)S(1)}, f32[16,256]{1,0:T(8,128)S(1)}, u32[]{:S(2)}, u32[]{:S(2)}) collective-permute-start(f32[16,256]{1,0:T(8,128)S(1)} %shard_map.127.refs_8_), channel_id=1, source_target_pairs={{0,48},{16,0},{32,16},{48,32},{1,49},{17,1},{33,17},{49,33},{2,50}... | collective-permute-start | bytes 49160 | tf_op jit(solution)/shard_map/ppermute | solution.py:28
  44.1 1.0 copy-start.2
  45.1 0.9 copy-start.4
  52.9 7.9 %copy-start.5 = (f32[64,640]{1,0:T(8,128)}, f32[64,640]{1,0:T(8,128)S(1)}, u32[]{:S(2)}) copy-start(f32[64,640]{1,0:T(8,128)S(1)} %get-tuple-element.18) | copy-start | bytes 491524
  52.9 7.9 %copy-start.6 = (bf16[512,640]{1,0:T(8,128)(2,1)}, bf16[512,640]{1,0:T(8,128)(2,1)S(1)}, u32[]{:S(2)}) copy-start(bf16[512,640]{1,0:T(8,128)(2,1)S(1)} %get-tuple-element.17) | copy-start | bytes 1966084
  52.9 9.9 %collective-permute-start.13 = (bf16[64,640]{1,0:T(8,128)(2,1)}, bf16[64,640]{1,0:T(8,128)(2,1)S(1)}, u32[]{:S(2)}, u32[]{:S(2)}) collective-permute-start(bf16[64,640]{1,0:T(8,128)(2,1)} %get-tuple-element.21), channel_id=1, source_target_pairs={{0,16},{16,32},{32,48},{48,0},{1,17},{17,33},{33,49},{49,1},{2,18}... | collective-permute-start | bytes 245768 | tf_op jit(solution)/shard_map/ppermute | solution.py:28
  54.6 8.9 %collective-permute-start.12 = (bf16[64,640]{1,0:T(8,128)(2,1)S(1)}, bf16[64,640]{1,0:T(8,128)(2,1)S(1)}, u32[]{:S(2)}, u32[]{:S(2)}) collective-permute-start(bf16[64,640]{1,0:T(8,128)(2,1)S(1)} %get-tuple-element.20), channel_id=1, source_target_pairs={{0,32},{16,48},{32,0},{48,16},{1,33},{17,49},{33,1},{49,17},{2,34}... | collective-permute-start | bytes 245768 | tf_op jit(solution)/shard_map/ppermute | solution.py:28
  58.7 6.5 %collective-permute-start.11 = (bf16[64,640]{1,0:T(8,128)(2,1)S(1)}, bf16[64,640]{1,0:T(8,128)(2,1)S(1)}, u32[]{:S(2)}, u32[]{:S(2)}) collective-permute-start(bf16[64,640]{1,0:T(8,128)(2,1)S(1)} %get-tuple-element.19), channel_id=1, source_target_pairs={{0,48},{16,0},{32,16},{48,32},{1,49},{17,1},{33,17},{49,33},{2,50}... | collective-permute-start | bytes 245768 | tf_op jit(solution)/shard_map/ppermute | solution.py:28
  60.8 24.5 %collective-permute-start.17 = (bf16[640,384]{1,0:T(8,128)(2,1)}, bf16[640,384]{1,0:T(8,128)(2,1)S(1)}, u32[]{:S(2)}, u32[]{:S(2)}) collective-permute-start(bf16[640,384]{1,0:T(8,128)(2,1)} %get-tuple-element.40), channel_id=1, source_target_pairs={{0,4},{4,0},{1,5},{5,1},{2,6},{6,2},{3,7},{7,3},{8,12},{12,8},{9,1... | collective-permute-start | bytes 1474568 | tf_op jit(solution)/shard_map/ppermute | solution.py:32
  60.8 7.2 %collective-permute-start.9 = (bf16[512,640]{1,0:T(8,128)(2,1)}, bf16[512,640]{1,0:T(8,128)(2,1)S(1)}, u32[]{:S(2)}, u32[]{:S(2)}) collective-permute-start(bf16[512,640]{1,0:T(8,128)(2,1)} %copy-done.6), channel_id=1, source_target_pairs={{0,4},{4,0},{1,5},{5,1},{2,6},{6,2},{3,7},{7,3},{8,12},{12,8},{9,1... | collective-permute-start | bytes 1966088 | tf_op jit(solution)/shard_map/ppermute | solution.py:32
  68.1 1.1 copy-start.7
  69.2 7.5 %collective-permute-start.10 = (bf16[256,640]{1,0:T(8,128)(2,1)S(1)}, bf16[256,640]{1,0:T(8,128)(2,1)}, u32[]{:S(2)}, u32[]{:S(2)}) collective-permute-start(bf16[256,640]{1,0:T(8,128)(2,1)S(1)} %fusion.13), channel_id=1, source_target_pairs={{0,8},{8,0},{1,9},{9,1},{2,10},{10,2},{3,11},{11,3},{4,12},{12,4},... | collective-permute-start | bytes 983048 | tf_op jit(solution)/shard_map/ppermute | solution.py:32
  75.1 2.9 %copy-start.9 = (bf16[1280,640]{0,1:T(8,128)(2,1)S(1)}, bf16[1280,640]{0,1:T(8,128)(2,1)}, u32[]{:S(2)}) copy-start(bf16[1280,640]{0,1:T(8,128)(2,1)} %copy-done.8) | copy-start | bytes 4915204
  78.0 1.3 copy-start.14
  78.6 1.9 %copy-start.13 = (bf16[64,320]{0,1:T(8,128)(2,1)S(1)}, bf16[64,320]{0,1:T(8,128)(2,1)}, u32[]{:S(2)}) copy-start(bf16[64,320]{0,1:T(8,128)(2,1)} %copy.23) | copy-start | bytes 122884
  79.2 4.0 %copy-start.12 = (bf16[64,320]{0,1:T(8,128)(2,1)S(1)}, bf16[64,320]{0,1:T(8,128)(2,1)}, u32[]{:S(2)}) copy-start(bf16[64,320]{0,1:T(8,128)(2,1)} %copy.22) | copy-start | bytes 122884
  79.3 10.8 %collective-permute-start.16 = (bf16[320,320]{0,1:T(8,128)(2,1)S(1)}, bf16[320,320]{0,1:T(8,128)(2,1)S(1)}, u32[]{:S(2)}, u32[]{:S(2)}) collective-permute-start(bf16[320,320]{0,1:T(8,128)(2,1)S(1)} %pad_maximum_fusion.3), channel_id=1, source_target_pairs={{0,3},{1,0},{2,1},{3,2},{4,7},{5,4},{6,5},{7,6},{8,11},{9,8},{10,9... | collective-permute-start | bytes 614408 | tf_op jit(solution)/shard_map/ppermute | solution.py:28
  79.9 5.4 %collective-permute-start.18 = (bf16[320,640]{1,0:T(8,128)(2,1)S(1)}, bf16[320,640]{1,0:T(8,128)(2,1)S(1)}, u32[]{:S(2)}, u32[]{:S(2)}) collective-permute-start(bf16[320,640]{1,0:T(8,128)(2,1)S(1)} %pad_maximum_fusion.y_ref), channel_id=1, source_target_pairs={{0,4},{4,0},{1,5},{5,1},{2,6},{6,2},{3,7},{7,3},{8,12},{12,8},{9,1... | collective-permute-start | bytes 1228808 | tf_op jit(solution)/shard_map/ppermute | solution.py:32
  80.5 11.4 %collective-permute-start.15 = (bf16[320,320]{0,1:T(8,128)(2,1)S(1)}, bf16[320,320]{0,1:T(8,128)(2,1)S(1)}, u32[]{:S(2)}, u32[]{:S(2)}) collective-permute-start(bf16[320,320]{0,1:T(8,128)(2,1)S(1)} %pad_maximum_fusion.2), channel_id=1, source_target_pairs={{0,2},{1,3},{2,0},{3,1},{4,6},{5,7},{6,4},{7,5},{8,10},{9,11},{10,... | collective-permute-start | bytes 614408 | tf_op jit(solution)/shard_map/ppermute | solution.py:28
  83.3 12.6 %collective-permute-start.14 = (bf16[320,320]{0,1:T(8,128)(2,1)S(1)}, bf16[320,320]{0,1:T(8,128)(2,1)S(1)}, u32[]{:S(2)}, u32[]{:S(2)}) collective-permute-start(bf16[320,320]{0,1:T(8,128)(2,1)S(1)} %pad_maximum_fusion.1), channel_id=1, source_target_pairs={{0,1},{1,2},{2,3},{3,0},{4,5},{5,6},{6,7},{7,4},{8,9},{9,10},{10,1... | collective-permute-start | bytes 614408 | tf_op jit(solution)/shard_map/ppermute | solution.py:28
  86.6 20.4 %collective-permute-start.21 = (bf16[160,1280]{1,0:T(8,128)(2,1)S(1)}, bf16[160,1280]{1,0:T(8,128)(2,1)S(1)}, u32[]{:S(2)}, u32[]{:S(2)}) collective-permute-start(bf16[160,1280]{1,0:T(8,128)(2,1)S(1)} %get-tuple-element.25), channel_id=1, source_target_pairs={{0,192},{64,0},{128,64},{192,128},{1,193},{65,1},{129,65},{193,129... | collective-permute-start | bytes 1228808 | tf_op jit(solution)/shard_map/ppermute | solution.py:28
  89.3 17.7 %collective-permute-start.20 = (bf16[160,1280]{1,0:T(8,128)(2,1)S(1)}, bf16[160,1280]{1,0:T(8,128)(2,1)S(1)}, u32[]{:S(2)}, u32[]{:S(2)}) collective-permute-start(bf16[160,1280]{1,0:T(8,128)(2,1)S(1)} %get-tuple-element.24), channel_id=1, source_target_pairs={{0,128},{64,192},{128,0},{192,64},{1,129},{65,193},{129,1},{193,65... | collective-permute-start | bytes 1228808 | tf_op jit(solution)/shard_map/ppermute | solution.py:28
  90.1 20.5 %collective-permute-start.19 = (bf16[160,1280]{1,0:T(8,128)(2,1)S(1)}, bf16[160,1280]{1,0:T(8,128)(2,1)S(1)}, u32[]{:S(2)}, u32[]{:S(2)}) collective-permute-start(bf16[160,1280]{1,0:T(8,128)(2,1)S(1)} %get-tuple-element.23), channel_id=1, source_target_pairs={{0,64},{64,128},{128,192},{192,0},{1,65},{65,129},{129,193},{193,1... | collective-permute-start | bytes 1228808 | tf_op jit(solution)/shard_map/ppermute | solution.py:28
  110.8 7.1 %collective-permute-start.22 = (bf16[80,1280]{1,0:T(8,128)(2,1)S(1)}, bf16[80,1280]{1,0:T(8,128)(2,1)S(1)}, u32[]{:S(2)}, u32[]{:S(2)}) collective-permute-start(bf16[80,1280]{1,0:T(8,128)(2,1)S(1)} %slice.125), channel_id=1, source_target_pairs={{0,8},{8,0},{1,9},{9,1},{2,10},{10,2},{3,11},{11,3},{4,12},{12,4},... | collective-permute-start | bytes 614408 | tf_op jit(solution)/shard_map/ppermute | solution.py:32
  118.0 7.0 %collective-permute-start.25 = (bf16[20,1280]{1,0:T(8,128)(2,1)S(1)}, bf16[20,1280]{1,0:T(8,128)(2,1)S(1)}, u32[]{:S(2)}, u32[]{:S(2)}) collective-permute-start(bf16[20,1280]{1,0:T(8,128)(2,1)S(1)} %get-tuple-element.43), channel_id=1, source_target_pairs={{0,48},{16,0},{32,16},{48,32},{1,49},{17,1},{33,17},{49,33},{2,50}... | collective-permute-start | bytes 153608 | tf_op jit(solution)/shard_map/ppermute | solution.py:28
  121.0 9.1 %collective-permute-start.24 = (bf16[20,1280]{1,0:T(8,128)(2,1)S(1)}, bf16[20,1280]{1,0:T(8,128)(2,1)S(1)}, u32[]{:S(2)}, u32[]{:S(2)}) collective-permute-start(bf16[20,1280]{1,0:T(8,128)(2,1)S(1)} %get-tuple-element.44), channel_id=1, source_target_pairs={{0,32},{16,48},{32,0},{48,16},{1,33},{17,49},{33,1},{49,17},{2,34}... | collective-permute-start | bytes 153608 | tf_op jit(solution)/shard_map/ppermute | solution.py:28
  124.3 6.5 %collective-permute-start.23 = (bf16[20,1280]{1,0:T(8,128)(2,1)S(1)}, bf16[20,1280]{1,0:T(8,128)(2,1)S(1)}, u32[]{:S(2)}, u32[]{:S(2)}) collective-permute-start(bf16[20,1280]{1,0:T(8,128)(2,1)S(1)} %get-tuple-element.42), channel_id=1, source_target_pairs={{0,16},{16,32},{32,48},{48,0},{1,17},{17,33},{33,49},{49,1},{2,18}... | collective-permute-start | bytes 153608 | tf_op jit(solution)/shard_map/ppermute | solution.py:28

commit v2 on v1

--- a/solution.py
+++ b/solution.py
@@ -69,8 +69,8 @@
 
 def grads_kernel(heads, valid_ref, *refs):
     rows_refs, frame_refs, stat_refs = refs[:4], refs[4:8], refs[8:12]
-    keep_ref, send_ref = refs[12:14]
-    dq_refs = refs[14:18]
+    keep_refs, send_ref = refs[12:14], refs[14]
+    dq_refs = refs[15:19]
     width = heads * HD
     rows = jnp.concatenate([r[...] for r in rows_refs], axis=0)
     blocks = [r[...] for r in frame_refs]
@@ -104,8 +104,8 @@
             probs = probs.astype(BF)
             dkey = mm(dscores, query) * SCALE
             dvalue = mm(probs, dout)
-            out_ref = send_ref if j % 2 else keep_ref
-            span = slice((j // 2) * part, (j // 2 + 1) * part)
+            out_ref = send_ref if j % 2 else keep_refs[j // 2]
+            span = slice((j // 2) * part, (j // 2 + 1) * part) if j % 2 else slice(0, part)
             out_ref[span, cut] = dkey.astype(out_ref.dtype)
             out_ref[span, cut2] = dvalue.astype(out_ref.dtype)
             dq_sum += mm(key, dscores, TN)
@@ -117,30 +117,63 @@
         dq_refs[k][...] = joined[k * own : (k + 1) * own].astype(dq_refs[k].dtype)
 
 
+def project_kernel(left_ref, right_ref, w1_ref, w2_ref, out_ref):
+    width = w1_ref.shape[0]
+    out_ref[:, :width] = mm(left_ref[...], w1_ref[...], NT).astype(out_ref.dtype)
+    out_ref[:, width:] = mm(right_ref[...], w2_ref[...], NT).astype(out_ref.dtype)
+
+
+def frames_kernel(frames_ref, w1_ref, w2_ref, out_ref):
+    project_kernel(frames_ref, frames_ref, w1_ref, w2_ref, out_ref)
+
+
+def collect_kernel(keep_ref, core_ref, pair_ref, dq_ref, a_ref, b_ref, c_ref, out_ref):
+    slab = keep_ref.shape[0]
+    total = keep_ref[...] + core_ref[:slab].astype(F32) + pair_ref[...].astype(F32)
+    out_ref[:slab] = total.astype(out_ref.dtype)
+    total = dq_ref[...] + a_ref[...].astype(F32) + b_ref[...].astype(F32)
+    out_ref[slab:] = (total + c_ref[...].astype(F32)).astype(out_ref.dtype)
+
+
 def weights_kernel(part, xt_ref, xt2_ref, y_ref, y2_ref, *out_refs):
+    kv_refs, keep_ref, send_ref = out_refs[:4], out_refs[4], out_refs[5]
     frames = y_ref.shape[0] - part
     half = y_ref.shape[1] // 2
-    step = out_refs[0].shape[0]
+    step = kv_refs[0].shape[0]
     pairs = ((xt_ref, y_ref), (xt2_ref, y2_ref))
-    for k, out_ref in enumerate(out_refs):
+    for k in (3, 1, 2, 0):
         span = slice(k * step, (k + 1) * step)
         kv = sum(mm(x[span, :frames], y[:frames, :]) for x, y in pairs)
+        kv_refs[k][...] = kv.astype(kv_refs[k].dtype)
         q = sum(
-            mm(x[span, frames : frames + part], y[frames : frames + part, :half])
-            for x, y in pairs
+            mm(x[span, frames : frames + part], y[frames:, :half]) for x, y in pairs
         )
-        o = sum(
-            mm(x[span, frames + part :], y[frames : frames + part, half:])
-            for x, y in pairs
-        )
-        out_ref[:, : 2 * half] = kv.astype(out_ref.dtype)
-        out_ref[:, 2 * half : 3 * half] = q.astype(out_ref.dtype)
-        out_ref[:, 3 * half :] = o.astype(out_ref.dtype)
+        o = sum(mm(x[span, frames + part :], y[frames:, half:]) for x, y in pairs)
+        near = slice(k * step // 2, (k + 1) * step // 2)
+        keep_ref[near, :half] = q[: step // 2]
+        keep_ref[near, half:] = o[: step // 2]
+        send_ref[near, :half] = q[step // 2 :].astype(send_ref.dtype)
+        send_ref[near, half:] = o[step // 2 :].astype(send_ref.dtype)
+
+
+def inputs_kernel(where_ref, y_ref, wk_ref, wv_ref, wq_ref, own_ref, *refs):
+    send_refs, scratch = refs[:3], refs[3]
+    width = wk_ref.shape[0]
+    frames = y_ref.shape[0] - (y_ref.shape[0] // 5)
+    dkey, dvalue = y_ref[:frames, :width], y_ref[:frames, width:]
+    dquery = y_ref[frames:, :width]
+    for t in range(4):
+        span = slice(t * width, (t + 1) * width)
+        scratch[t, :frames] = mm(dkey, wk_ref[:, span]) + mm(dvalue, wv_ref[:, span])
+        scratch[t, frames:] = mm(dquery, wq_ref[:, span])
+    own_ref[...] = scratch[where_ref[0]]
+    for k in (1, 2, 3):
+        send_refs[k - 1][...] = scratch[lax.rem(where_ref[0] + k, 4)].astype(BF)
 
 
 VMEM = pl.BlockSpec(memory_space=pltpu.VMEM)
 SMEM = pl.BlockSpec(memory_space=pltpu.SMEM)
-PARAMS = pltpu.CompilerParams(vmem_limit_bytes=48 * 1024 * 1024)
+PARAMS = pltpu.CompilerParams(vmem_limit_bytes=24 * 1024 * 1024)
 
 
 def per_device(query_in, grad_out, encoder_states, frame_lengths, w_query, w_key, w_value, w_out):
@@ -151,15 +184,31 @@
     own, slab = rows_in.shape[0], frames.shape[0]
     xi, ai, bi, ci, yi = (lax.axis_index(n) for n in ("dp", "a", "b", "core", "head"))
 
-    query = mm(rows_in, w_query).astype(BF)
-    dout = mm(rows_grad, w_out, NT).astype(BF)
-    rows0 = jnp.concatenate([query, dout], axis=1)
-    row_blocks = [rows0] + [ring(rows0, "a", 4, j) for j in (1, 2, 3)]
-
-    w_kv = jnp.concatenate([w_key, w_value], axis=1)
-    kv = mm(frames, w_kv).astype(BF)
+    wq_t, wk_t, wv_t = w_query.T, w_key.T, w_value.T
+    rows0 = pl.pallas_call(
+        project_kernel,
+        out_shape=jax.ShapeDtypeStruct((own, 2 * width), BF),
+        in_specs=[VMEM] * 4,
+        out_specs=VMEM,
+        compiler_params=PARAMS,
+    )(rows_in, rows_grad, wq_t, w_out)
+    row_blocks = [rows0] + [ring(rows0, "a", 4, j) for j in (2, 1, 3)]
+
+    frames, rows0 = lax.optimization_barrier((frames, rows0))
+    kv = pl.pallas_call(
+        frames_kernel,
+        out_shape=jax.ShapeDtypeStruct((slab, 2 * width), BF),
+        in_specs=[VMEM] * 3,
+        out_specs=VMEM,
+        compiler_params=PARAMS,
+    )(frames, wk_t, wv_t)
     kv_pair = swap(kv, "b")
-    frame_blocks = [kv, swap(kv, "core"), kv_pair, swap(kv_pair, "core")]
+    kv_core = swap(kv, "core")
+    row_blocks[1:], kv_pair, kv_core = lax.optimization_barrier(
+        (row_blocks[1:], kv_pair, kv_core)
+    )
+    row_blocks = [rows0, row_blocks[2], row_blocks[1], row_blocks[3]]
+    frame_blocks = [kv, kv_core, kv_pair, swap(kv_pair, "core")]
     starts = [
         slab * (4 * ai + 2 * (bi ^ db) + (ci ^ dc)) for db in (0, 1) for dc in (0, 1)
     ]
@@ -188,59 +237,75 @@
     )(valid, *row_blocks, *frame_blocks)
     all_stats = [stats] + [ring(stats, "a", 4, j) for j in (1, 2, 3)]
 
-    keep, send, dq0, dq1, dq2, dq3 = pl.pallas_call(
+    keep0, keep1, send, dq0, dq1, dq2, dq3 = pl.pallas_call(
         functools.partial(grads_kernel, heads),
-        out_shape=[
-            jax.ShapeDtypeStruct((2 * slab, 2 * width), F32),
+        out_shape=[jax.ShapeDtypeStruct((slab, 2 * width), F32)] * 2
+        + [
             jax.ShapeDtypeStruct((2 * slab, 2 * width), BF),
             jax.ShapeDtypeStruct((own, 2 * width), F32),
         ]
         + [jax.ShapeDtypeStruct((own, 2 * width), BF)] * 3,
         in_specs=[SMEM] + [VMEM] * 12,
+        out_specs=[VMEM] * 7,
+        compiler_params=PARAMS,
+    )(valid, *row_blocks, *frame_blocks, *all_stats)
+
+    recv = swap(send, "core")
+    pair = (keep1 + recv[slab:].astype(F32)).astype(BF)
+    dq2, dq1, dq3, pair = lax.optimization_barrier((dq2, dq1, dq3, pair))
+    pair_recv = swap(pair, "b")
+    dq_recv = [ring(d, "a", 4, -j) for j, d in ((2, dq2), (1, dq1), (3, dq3))]
+    grads = pl.pallas_call(
+        collect_kernel,
+        out_shape=jax.ShapeDtypeStruct((slab + own, 2 * width), BF),
+        in_specs=[VMEM] * 7,
+        out_specs=VMEM,
+        compiler_params=PARAMS,
+    )(keep0, recv, pair_recv, dq0, *dq_recv)
+    grads_other = swap(grads, "core")
+
+    step = model // 8
+    *kv_parts, qo_keep, qo_send = pl.pallas_call(
+        functools.partial(weights_kernel, own),
+        out_shape=[jax.ShapeDtypeStruct((step, 2 * width), F32)]
+        + [jax.ShapeDtypeStruct((step, 2 * width), BF)] * 3
+        + [
+            jax.ShapeDtypeStruct((model // 4, 2 * width), F32),
+            jax.ShapeDtypeStruct((model // 4, 2 * width), BF),
+        ],
+        in_specs=[VMEM] * 4,
         out_specs=[VMEM] * 6,
         compiler_params=PARAMS,
-    )(valid, *row_blocks, *frame_blocks, *all_stats)
-
-    recv = swap(send, "core").astype(F32)
-    pair = (keep[slab:] + recv[slab:]).astype(BF)
-    pair_recv = swap(pair, "b").astype(F32)
-    dq_recv = [ring(d, "a", 4, -j).astype(F32) for j, d in ((1, dq1), (2, dq2), (3, dq3))]
-    dkv = (keep[:slab] + recv[:slab] + pair_recv).astype(BF)
-    dqo = (dq0 + dq_recv[0] + dq_recv[1] + dq_recv[2]).astype(BF)
-    grads = jnp.concatenate([dkv, dqo], axis=0)
-    grads_other = swap(grads, "core")
-
-    parts = []
-    for k in range(4):
-        start = ((yi + k) % 4) * width
-        w_kv_rows = lax.dynamic_slice_in_dim(w_kv, start, width, 0)
-        w_q_rows = lax.dynamic_slice_in_dim(w_query, start, width, 0)
-        parts.append(
-            jnp.concatenate(
-                [mm(dkv, w_kv_rows, NT), mm(dqo[:, :width], w_q_rows, NT)], axis=0
-            ).astype(BF if k else F32)
-        )
-    arrived = [ring(parts[k], "head", 4, k).astype(F32) for k in (1, 2, 3)]
-    inputs = (parts[0] + arrived[0] + arrived[1] + arrived[2]).astype(BF)
+    )(turned_own, turned_other, grads, grads_other)
+    kv_x = [ring(kv_parts[k], "dp", 4, k) for k in (2, 1, 3)]
+    qo_b = swap(qo_send, "b")
+
+    held, kv_parts[0] = lax.optimization_barrier((grads, kv_parts[0]))
+    own_part, *parts = pl.pallas_call(
+        inputs_kernel,
+        out_shape=[jax.ShapeDtypeStruct((slab + own, width), F32)]
+        + [jax.ShapeDtypeStruct((slab + own, width), BF)] * 3,
+        in_specs=[SMEM] + [VMEM] * 4,
+        out_specs=[VMEM] * 4,
+        scratch_shapes=[pltpu.VMEM((4, slab + own, width), F32)],
+        compiler_params=PARAMS,
+    )(yi.reshape(1).astype(jnp.int32), held, wk_t, wv_t, wq_t)
+    arrived = [ring(parts[k - 1], "head", 4, k) for k in (2, 1, 3)]
+
+    cut = step // 2
+    kv_sum = kv_parts[0] + sum(k.astype(F32) for k in kv_x)
+    qo_sum = qo_keep + qo_b.astype(F32)
+    kv_b = swap(kv_sum[cut:].astype(BF), "b")
+    qo_x = [ring(qo_sum[k * cut : (k + 1) * cut].astype(BF), "dp", 4, k) for k in (2, 1, 3)]
+    inputs = (own_part + sum(p.astype(F32) for p in arrived)).astype(BF)
     dframes, dinput = inputs[:slab], inputs[slab:]
 
-    step = model // 8
-    pieces = pl.pallas_call(
-        functools.partial(weights_kernel, own),
-        out_shape=[jax.ShapeDtypeStruct((step, 4 * width), F32)]
-        + [jax.ShapeDtypeStruct((step, 4 * width), BF)] * 3,
-        in_specs=[VMEM] * 4,
-        out_specs=[VMEM] * 4,
-        compiler_params=PARAMS,
-    )(turned_own, turned_other, grads, grads_other)
-    over_x = [ring(pieces[k], "dp", 4, k).astype(F32) for k in (1, 2, 3)]
-    total = pieces[0] + over_x[0] + over_x[1] + over_x[2]
-    total = total[: step // 2] + swap(total[step // 2 :].astype(BF), "b").astype(F32)
+    kv_sum = kv_sum[:cut] + kv_b.astype(F32)
+    qo_sum = qo_sum[:cut] + sum(q.astype(F32) for q in qo_x)
+    total = jnp.concatenate([kv_sum, qo_sum], axis=1)
     low = total.astype(BF)
-    over_a = [
-        ring(low[k * inner : (k + 1) * inner], "a", 4, k).astype(F32) for k in (1, 2, 3)
-    ]
-    total = total[:inner] + over_a[0] + over_a[1] + over_a[2]
+    over_a = [ring(low[k * inner : (k + 1) * inner], "a", 4, k) for k in (2, 1, 3)]
+    total = total[:inner] + sum(p.astype(F32) for p in over_a)
     return (
         dinput[None],
         dframes[None],

time: 132 us -> 126 us (0.955)
  matrix products: 8.95 us -> 3.22 us
  waiting for transfers between devices: 48.2 us -> 43.4 us
  Pallas kernels: 10.7 us -> 14.9 us
    ppermute x8 -> x9, waiting for transfers between devices: 14 us -> 2.61 us  [swap(): return lax.ppermute(x, axis, [(0, 1), (1, 0)])]
    ppermute x18 -> x21, waiting for transfers between devices: 34.2 us -> 40.8 us  [ring(): return lax.ppermute(x, axis, [(i, (i + step) % size) for i in range(size)])]
    unnamed x38 -> x41, local copies, waits for them, and re-layouts: 5.29 us -> 11.4 us
    dot_general x12 -> x1, matrix products: 8.95 us -> 3.22 us  [mm(): return lax.dot_general(left, right, dims, preferred_element_type=F32)]
    another operation x3 -> x0, local copies, waits for them, and re-layouts: 4.6 us -> none
    pallas_call x0 -> x4, Pallas kernels: none -> 3.2 us  [the longest x1 1.53 us: per_device(): pl.pallas_call(inputs_kernel, out_shape=[jax.ShapeDtypeStruct((slab + own...]
    ppermute x8 -> x9, starting transfers between devices: 3.87 us -> 6.36 us  [swap(): return lax.ppermute(x, axis, [(0, 1), (1, 0)])]
    convert_element_type x5 -> x2, other arithmetic: 2.48 us -> 0.19 us  [the longest x1 0.13 us: per_device(): inputs = (own_part + sum((p.astype(F32) for p in arrived))).astype(BF)]
  transfers between devices with their start and end apart: 26 -> 30, of which waited for: 15 -> 16; matrix products, arithmetic and copies ran while one was open for 14% -> 5% of each run, Pallas kernels for 1% -> 1%
where the time goes in v2:
time: 126 us; the launch traced here: 125 us
  starting transfers between devices  47.4 us (38%)
  waiting for transfers between devices  43.4 us (34%)
  Pallas kernels  14.9 us (12%)
  local copies, waits for them, and re-layouts  13 us (10%)
  matrix products  3.22 us (3%)
  other arithmetic  1.75 us (1%)
  between operations  1.59 us (1%)
    ppermute x21, starting transfers between devices, ring(): return lax.ppermute(x, axis, [(i, (i + step) % size) for i in range(size)])  41.1 us
    ppermute x21, waiting for transfers between devices, ring(): return lax.ppermute(x, axis, [(i, (i + step) % size) for i in range(size)])  40.8 us
    unnamed x41, local copies, waits for them, and re-layouts  11.4 us
    pallas_call x1, Pallas kernels, per_device(): pl.pallas_call(functools.partial(grads_kernel, heads), out_shape=[jax.Sha...  7.14 us
    ppermute x9, starting transfers between devices, swap(): return lax.ppermute(x, axis, [(0, 1), (1, 0)])  6.36 us
    dot_general x1, matrix products, mm(): return lax.dot_general(left, right, dims, preferred_element_type=F32)  3.22 us
    ppermute x9, waiting for transfers between devices, swap(): return lax.ppermute(x, axis, [(0, 1), (1, 0)])  2.61 us
  transfers between devices with their start and end apart: 30, of which 16 were waited for; matrix products, arithmetic and copies ran while one was open for 5% of the time, Pallas kernels for 1%

profile of v2, /device:TPU:8, one launch (start us, length us, event | category | flops | bytes accessed | tf_op | source)
XLA Modules:
  0.0 125.3 jit_solution(3447613189289952435)
XLA Ops:
  0.6 1.1 copy-done.2
  1.8 1.1 copy-done.6
  2.9 0.9 copy-done.14
  3.8 0.9 copy-done.15
  6.2 1.1 copy-done.7
  7.2 0.9 shard_map.128.refs_4_
  8.1 2.0 %collective-permute-start.3 = (bf16[256,640]{1,0:T(8,128)(2,1)S(1)}, bf16[256,640]{1,0:T(8,128)(2,1)S(1)}, u32[]{:S(2)}, u32[]{:S(2)}) collective-permute-start(bf16[256,640]{1,0:T(8,128)(2,1)S(1)} %shard_map.128.refs_4_), channel_id=1, source_target_pairs={{0,8},{8,0},{1,9},{9,1},{2,10},{10,2},{3,11},{11,3},{4,12},{12,4},... | collective-permute-start | bytes 983048 | tf_op jit(solution)/shard_map/ppermute | solution.py:32
  10.2 6.3 %collective-permute-start = (bf16[64,640]{1,0:T(8,128)(2,1)S(1)}, bf16[64,640]{1,0:T(8,128)(2,1)S(1)}, u32[]{:S(2)}, u32[]{:S(2)}) collective-permute-start(bf16[64,640]{1,0:T(8,128)(2,1)S(1)} %shard_map.127.refs_0_), channel_id=1, source_target_pairs={{0,32},{16,48},{32,0},{48,16},{1,33},{17,49},{33,1},{49,17},{2,34}... | collective-permute-start | bytes 245768 | tf_op jit(solution)/shard_map/ppermute | solution.py:28
  16.4 1.5 %collective-permute-start.1 = (bf16[64,640]{1,0:T(8,128)(2,1)S(1)}, bf16[64,640]{1,0:T(8,128)(2,1)S(1)}, u32[]{:S(2)}, u32[]{:S(2)}) collective-permute-start(bf16[64,640]{1,0:T(8,128)(2,1)S(1)} %shard_map.127.refs_0_), channel_id=1, source_target_pairs={{0,16},{16,32},{32,48},{48,0},{1,17},{17,33},{33,49},{49,1},{2,18}... | collective-permute-start | bytes 245768 | tf_op jit(solution)/shard_map/ppermute | solution.py:28
  17.9 2.7 %collective-permute-start.2 = (bf16[64,640]{1,0:T(8,128)(2,1)S(1)}, bf16[64,640]{1,0:T(8,128)(2,1)S(1)}, u32[]{:S(2)}, u32[]{:S(2)}) collective-permute-start(bf16[64,640]{1,0:T(8,128)(2,1)S(1)} %shard_map.127.refs_0_), channel_id=1, source_target_pairs={{0,48},{16,0},{32,16},{48,32},{1,49},{17,1},{33,17},{49,33},{2,50}... | collective-permute-start | bytes 245768 | tf_op jit(solution)/shard_map/ppermute | solution.py:28
  20.6 9.2 %collective-permute-done.refs_2_ = bf16[64,640]{1,0:T(8,128)(2,1)S(1)} collective-permute-done((bf16[64,640]{1,0:T(8,128)(2,1)S(1)}, bf16[64,640]{1,0:T(8,128)(2,1)S(1)}, u32[]{:S(2)}, u32[]{:S(2)}) %collective-permute-start) | collective-permute-done | bytes 81952 | tf_op jit(solution)/shard_map/ppermute | solution.py:28
  30.9 0.9 collective-permute-done.5.refs_7_
  31.7 2.5 %shard_map.129.refs_8_ = f32[16,256]{1,0:T(8,128)S(1)} custom-call(s32[4]{0:T(128)S(1)} %pad_add_fusion.valid_ref, bf16[64,640]{1,0:T(8,128)(2,1)S(1)} %shard_map.127.refs_0_, bf16[64,640]{1,0:T(8,128)(2,1)S(1)} %collective-permute-done.1.refs_1_, bf16[64,640]{1,0:T(8,128)(2,1)S(1)} %collective-permute-done.refs_2_, ...), custom_call_target="tpu_custom_call" | custom-call | tf_op jit(solution)/shard_map/pallas_call | solution.py:231
  34.2 1.2 collective-permute-start.6
  35.4 2.7 %collective-permute-start.7 = (f32[16,256]{1,0:T(8,128)S(1)}, f32[16,256]{1,0:T(8,128)S(1)}, u32[]{:S(2)}, u32[]{:S(2)}) collective-permute-start(f32[16,256]{1,0:T(8,128)S(1)} %shard_map.129.refs_8_), channel_id=1, source_target_pairs={{0,32},{16,48},{32,0},{48,16},{1,33},{17,49},{33,1},{49,17},{2,34}... | collective-permute-start | bytes 49160 | tf_op jit(solution)/shard_map/ppermute | solution.py:28
  38.1 1.8 %collective-permute-start.8 = (f32[16,256]{1,0:T(8,128)S(1)}, f32[16,256]{1,0:T(8,128)S(1)}, u32[]{:S(2)}, u32[]{:S(2)}) collective-permute-start(f32[16,256]{1,0:T(8,128)S(1)} %shard_map.129.refs_8_), channel_id=1, source_target_pairs={{0,48},{16,0},{32,16},{48,32},{1,49},{17,1},{33,17},{49,33},{2,50}... | collective-permute-start | bytes 49160 | tf_op jit(solution)/shard_map/ppermute | solution.py:28
  40.2 2.9 %collective-permute-done.7.refs_10_ = f32[16,256]{1,0:T(8,128)S(1)} collective-permute-done((f32[16,256]{1,0:T(8,128)S(1)}, f32[16,256]{1,0:T(8,128)S(1)}, u32[]{:S(2)}, u32[]{:S(2)}) %collective-permute-start.7) | collective-permute-done | bytes 16416 | tf_op jit(solution)/shard_map/ppermute | solution.py:28
  43.1 7.1 %shard_map.130 = (f32[256,640]{1,0:T(8,128)S(1)}, f32[256,640]{1,0:T(8,128)S(1)}, bf16[512,640]{1,0:T(8,128)(2,1)}, f32[64,640]{1,0:T(8,128)S(1)}, bf16[64,640]{...) custom-call(s32[4]{0:T(128)S(1)} %pad_add_fusion.valid_ref, ...), custom_call_target="tpu_custom_call" | custom-call | tf_op jit(solution)/shard_map/pallas_call | solution.py:240
  50.2 0.9 copy-done.8
  51.1 0.9 copy-done.10
  53.2 3.2 %fusion.4 = bf16[1280,384]{1,0:T(8,128)(2,1)S(1)} fusion(s32[1280]{0:T(1024)S(1)} %fusion.30, bf16[64,1280]{1,0:T(8,128)(2,1)} %bitcast.32, bf16[64,1280]{1,0:T(8,128)(2,1)} %bitcast.30, bf16[256,1280]{1,0:T(8,128)(2,1)} %bitcast.28), kind=kOutput, calls=%fused_computation.4 | convolution fusion | flops 1265008640 | bytes 1971200 | tf_op jit(solution)/shard_map/dot_general | solution.py:24
  56.6 1.5 %collective-permute-start.10 = (bf16[256,640]{1,0:T(8,128)(2,1)S(1)}, bf16[256,640]{1,0:T(8,128)(2,1)S(1)}, u32[]{:S(2)}, u32[]{:S(2)}) collective-permute-start(bf16[256,640]{1,0:T(8,128)(2,1)S(1)} %add_convert_fusion), channel_id=1, source_target_pairs={{0,8},{8,0},{1,9},{9,1},{2,10},{10,2},{3,11},{11,3},{4,12},{12,4},... | collective-permute-start | bytes 983048 | tf_op jit(solution)/shard_map/ppermute | solution.py:32
  58.1 2.9 %collective-permute-start.11 = (bf16[64,640]{1,0:T(8,128)(2,1)S(1)}, bf16[64,640]{1,0:T(8,128)(2,1)S(1)}, u32[]{:S(2)}, u32[]{:S(2)}) collective-permute-start(bf16[64,640]{1,0:T(8,128)(2,1)S(1)} %copy-done.19), channel_id=1, source_target_pairs={{0,32},{16,48},{32,0},{48,16},{1,33},{17,49},{33,1},{49,17},{2,34}... | collective-permute-start | bytes 245768 | tf_op jit(solution)/shard_map/ppermute | solution.py:28
  61.0 3.5 %collective-permute-start.12 = (bf16[64,640]{1,0:T(8,128)(2,1)S(1)}, bf16[64,640]{1,0:T(8,128)(2,1)S(1)}, u32[]{:S(2)}, u32[]{:S(2)}) collective-permute-start(bf16[64,640]{1,0:T(8,128)(2,1)S(1)} %copy-done.17), channel_id=1, source_target_pairs={{0,48},{16,0},{32,16},{48,32},{1,49},{17,1},{33,17},{49,33},{2,50}... | collective-permute-start | bytes 245768 | tf_op jit(solution)/shard_map/ppermute | solution.py:28
  64.7 7.8 %collective-permute-done.11.a_ref = bf16[64,640]{1,0:T(8,128)(2,1)S(1)} collective-permute-done((bf16[64,640]{1,0:T(8,128)(2,1)S(1)}, bf16[64,640]{1,0:T(8,128)(2,1)S(1)}, u32[]{:S(2)}, u32[]{:S(2)}) %collective-permute-start.11) | collective-permute-done | bytes 81952 | tf_op jit(solution)/shard_map/ppermute | solution.py:28
  72.5 3.8 %collective-permute-done.13.c_ref = bf16[64,640]{1,0:T(8,128)(2,1)S(1)} collective-permute-done((bf16[64,640]{1,0:T(8,128)(2,1)S(1)}, bf16[64,640]{1,0:T(8,128)(2,1)S(1)}, u32[]{:S(2)}, u32[]{:S(2)}) %collective-permute-start.13) | collective-permute-done | bytes 81952 | tf_op jit(solution)/shard_map/ppermute | solution.py:28
  76.8 1.7 %collective-permute-done.15.y2_ref = bf16[320,640]{1,0:T(8,128)(2,1)S(1)} collective-permute-done((bf16[320,640]{1,0:T(8,128)(2,1)S(1)}, bf16[320,640]{1,0:T(8,128)(2,1)S(1)}, u32[]{:S(2)}, u32[]{:S(2)}) %collective-permute-start.15) | collective-permute-done | bytes 409632 | tf_op jit(solution)/shard_map/ppermute | solution.py:32
  78.5 2.1 %shard_map.132 = (f32[160,640]{1,0:T(8,128)S(1)}, bf16[160,640]{1,0:T(8,128)(2,1)}, bf16[160,640]{1,0:T(8,128)(2,1)}, bf16[160,640]{1,0:T(8,128)(2,1)}, f32[320,...) custom-call(bf16[640,384]{1,0:T(8,128)(2,1)S(1)} %get-tuple-element.75.xt_ref, ...), custom_call_target="tpu_custom_call" | custom-call | tf_op jit(solution)/shard_map/pallas_call | solution.py:268
  80.6 0.9 copy-done.4
  82.2 3.0 %collective-permute-start.19 = (bf16[160,640]{1,0:T(8,128)(2,1)}, bf16[160,640]{1,0:T(8,128)(2,1)}, u32[]{:S(2)}, u32[]{:S(2)}) collective-permute-start(bf16[160,640]{1,0:T(8,128)(2,1)} %get-tuple-element.61), channel_id=1, source_target_pairs={{0,128},{64,192},{128,0},{192,64},{1,129},{65,193},{129,1},{193,65... | collective-permute-start | bytes 614408 | tf_op jit(solution)/shard_map/ppermute | solution.py:28
  85.8 2.6 %collective-permute-start.21 = (bf16[160,640]{1,0:T(8,128)(2,1)}, bf16[160,640]{1,0:T(8,128)(2,1)}, u32[]{:S(2)}, u32[]{:S(2)}) collective-permute-start(bf16[160,640]{1,0:T(8,128)(2,1)} %get-tuple-element.63), channel_id=1, source_target_pairs={{0,192},{64,0},{128,64},{192,128},{1,193},{65,1},{129,65},{193,129... | collective-permute-start | bytes 614408 | tf_op jit(solution)/shard_map/ppermute | solution.py:28
  88.5 1.2 collective-permute-start.23
  89.6 1.5 %shard_map.133 = (f32[320,320]{1,0:T(8,128)S(1)}, bf16[320,320]{1,0:T(8,128)(2,1)S(1)}, bf16[320,320]{1,0:T(8,128)(2,1)S(1)}, bf16[320,320]{1,0:T(8,128)(2,1)S(1)}) custom-call(s32[1]{0:T(128)} %bitcast.where_ref, bf16[320,640]{1,0:T(8,128)(2,1)S(1)} %shard_map.131.y_ref, bf16[320,1280]{1,0:T(8,128)(2,1)S(1)} %bitcast.23, bf16[320,1280]{1,0:T(8,128)(2,1)S(1)} %bitcast.25, ...), custom_call_target="tpu_custom_call" | custom-call | tf_op jit(solution)/shard_map/pallas_call | solution.py:284
  91.2 2.3 %collective-permute-start.16 = (bf16[320,320]{1,0:T(8,128)(2,1)S(1)}, bf16[320,320]{1,0:T(8,128)(2,1)S(1)}, u32[]{:S(2)}, u32[]{:S(2)}) collective-permute-start(bf16[320,320]{1,0:T(8,128)(2,1)S(1)} %get-tuple-element.57), channel_id=1, source_target_pairs={{0,2},{1,3},{2,0},{3,1},{4,6},{5,7},{6,4},{7,5},{8,10},{9,11},{10,... | collective-permute-start | bytes 614408 | tf_op jit(solution)/shard_map/ppermute | solution.py:28
  93.6 2.0 %collective-permute-done.20 = bf16[160,640]{1,0:T(8,128)(2,1)} collective-permute-done((bf16[160,640]{1,0:T(8,128)(2,1)}, bf16[160,640]{1,0:T(8,128)(2,1)}, u32[]{:S(2)}, u32[]{:S(2)}) %collective-permute-start.20) | collective-permute-done | bytes 204832 | tf_op jit(solution)/shard_map/ppermute | solution.py:28
  96.0 1.2 add_add_fusion
  97.3 1.2 collective-permute-start.22
  98.5 1.6 %collective-permute-done.16 = bf16[320,320]{1,0:T(8,128)(2,1)S(1)} collective-permute-done((bf16[320,320]{1,0:T(8,128)(2,1)S(1)}, bf16[320,320]{1,0:T(8,128)(2,1)S(1)}, u32[]{:S(2)}, u32[]{:S(2)}) %collective-permute-start.16) | collective-permute-done | bytes 204832 | tf_op jit(solution)/shard_map/ppermute | solution.py:28
  100.0 5.0 %collective-permute-done.17 = bf16[320,320]{1,0:T(8,128)(2,1)S(1)} collective-permute-done((bf16[320,320]{1,0:T(8,128)(2,1)S(1)}, bf16[320,320]{1,0:T(8,128)(2,1)S(1)}, u32[]{:S(2)}, u32[]{:S(2)}) %collective-permute-start.17) | collective-permute-done | bytes 204832 | tf_op jit(solution)/shard_map/ppermute | solution.py:28
  105.5 1.1 collective-permute-start.25
  106.6 2.2 %collective-permute-start.26 = (bf16[80,640]{1,0:T(8,128)(2,1)S(1)}, bf16[80,640]{1,0:T(8,128)(2,1)S(1)}, u32[]{:S(2)}, u32[]{:S(2)}) collective-permute-start(bf16[80,640]{1,0:T(8,128)(2,1)S(1)} %get-tuple-element.77), channel_id=1, source_target_pairs={{0,192},{64,0},{128,64},{192,128},{1,193},{65,1},{129,65},{193,129... | collective-permute-start | bytes 307208 | tf_op jit(solution)/shard_map/ppermute | solution.py:28
  108.8 3.9 %collective-permute-done.24 = bf16[80,640]{1,0:T(8,128)(2,1)S(1)} collective-permute-done((bf16[80,640]{1,0:T(8,128)(2,1)S(1)}, bf16[80,640]{1,0:T(8,128)(2,1)S(1)}, u32[]{:S(2)}, u32[]{:S(2)}) %collective-permute-start.24) | collective-permute-done | bytes 102432 | tf_op jit(solution)/shard_map/ppermute | solution.py:28
  112.7 0.9 collective-permute-done.25
  113.8 1.9 %collective-permute-start.27 = (bf16[20,1280]{1,0:T(8,128)(2,1)S(1)}, bf16[20,1280]{1,0:T(8,128)(2,1)S(1)}, u32[]{:S(2)}, u32[]{:S(2)}) collective-permute-start(bf16[20,1280]{1,0:T(8,128)(2,1)S(1)} %get-tuple-element.79), channel_id=1, source_target_pairs={{0,32},{16,48},{32,0},{48,16},{1,33},{17,49},{33,1},{49,17},{2,34}... | collective-permute-start | bytes 153608 | tf_op jit(solution)/shard_map/ppermute | solution.py:28
  115.7 2.7 %collective-permute-start.28 = (bf16[20,1280]{1,0:T(8,128)(2,1)S(1)}, bf16[20,1280]{1,0:T(8,128)(2,1)S(1)}, u32[]{:S(2)}, u32[]{:S(2)}) collective-permute-start(bf16[20,1280]{1,0:T(8,128)(2,1)S(1)} %get-tuple-element.81), channel_id=1, source_target_pairs={{0,16},{16,32},{32,48},{48,0},{1,17},{17,33},{33,49},{49,1},{2,18}... | collective-permute-start | bytes 153608 | tf_op jit(solution)/shard_map/ppermute | solution.py:28
  118.4 1.4 %collective-permute-start.29 = (bf16[20,1280]{1,0:T(8,128)(2,1)S(1)}, bf16[20,1280]{1,0:T(8,128)(2,1)S(1)}, u32[]{:S(2)}, u32[]{:S(2)}) collective-permute-start(bf16[20,1280]{1,0:T(8,128)(2,1)S(1)} %get-tuple-element.80), channel_id=1, source_target_pairs={{0,48},{16,0},{32,16},{48,32},{1,49},{17,1},{33,17},{49,33},{2,50}... | collective-permute-start | bytes 153608 | tf_op jit(solution)/shard_map/ppermute | solution.py:28
  121.3 1.3 %collective-permute-done.27 = bf16[20,1280]{1,0:T(8,128)(2,1)S(1)} collective-permute-done((bf16[20,1280]{1,0:T(8,128)(2,1)S(1)}, bf16[20,1280]{1,0:T(8,128)(2,1)S(1)}, u32[]{:S(2)}, u32[]{:S(2)}) %collective-permute-start.27) | collective-permute-done | bytes 51232 | tf_op jit(solution)/shard_map/ppermute | solution.py:28
  122.8 1.7 %collective-permute-done.29 = bf16[20,1280]{1,0:T(8,128)(2,1)S(1)} collective-permute-done((bf16[20,1280]{1,0:T(8,128)(2,1)S(1)}, bf16[20,1280]{1,0:T(8,128)(2,1)S(1)}, u32[]{:S(2)}, u32[]{:S(2)}) %collective-permute-start.29) | collective-permute-done | bytes 51232 | tf_op jit(solution)/shard_map/ppermute | solution.py:28
  (78 shorter events, 8.9 us)
Async XLA Ops:
  0.6 1.1 copy-start.2
  1.8 1.1 copy-start.6
  2.9 0.9 copy-start.14
  3.8 0.9 copy-start.15
  4.8 1.1 copy-start
  4.8 1.4 %copy-start.1 = (bf16[1280,320]{0,1:T(8,128)(2,1)S(1)}, bf16[1280,320]{0,1:T(8,128)(2,1)}, u32[]{:S(2)}) copy-start(bf16[1280,320]{0,1:T(8,128)(2,1)} %param.14) | copy-start | bytes 2457604
  6.2 1.1 copy-start.7
  8.1 21.9 %collective-permute-start.3 = (bf16[256,640]{1,0:T(8,128)(2,1)S(1)}, bf16[256,640]{1,0:T(8,128)(2,1)S(1)}, u32[]{:S(2)}, u32[]{:S(2)}) collective-permute-start(bf16[256,640]{1,0:T(8,128)(2,1)S(1)} %shard_map.128.refs_4_), channel_id=1, source_target_pairs={{0,8},{8,0},{1,9},{9,1},{2,10},{10,2},{3,11},{11,3},{4,12},{12,4},... | collective-permute-start | bytes 983048 | tf_op jit(solution)/shard_map/ppermute | solution.py:32
  10.2 19.9 %collective-permute-start.4 = (bf16[256,640]{1,0:T(8,128)(2,1)S(1)}, bf16[256,640]{1,0:T(8,128)(2,1)S(1)}, u32[]{:S(2)}, u32[]{:S(2)}) collective-permute-start(bf16[256,640]{1,0:T(8,128)(2,1)S(1)} %shard_map.128.refs_4_), channel_id=1, source_target_pairs={{0,4},{4,0},{1,5},{5,1},{2,6},{6,2},{3,7},{7,3},{8,12},{12,8},{9,1... | collective-permute-start | bytes 983048 | tf_op jit(solution)/shard_map/ppermute | solution.py:32
  10.2 19.6 %collective-permute-start = (bf16[64,640]{1,0:T(8,128)(2,1)S(1)}, bf16[64,640]{1,0:T(8,128)(2,1)S(1)}, u32[]{:S(2)}, u32[]{:S(2)}) collective-permute-start(bf16[64,640]{1,0:T(8,128)(2,1)S(1)} %shard_map.127.refs_0_), channel_id=1, source_target_pairs={{0,32},{16,48},{32,0},{48,16},{1,33},{17,49},{33,1},{49,17},{2,34}... | collective-permute-start | bytes 245768 | tf_op jit(solution)/shard_map/ppermute | solution.py:28
  16.4 13.6 %collective-permute-start.1 = (bf16[64,640]{1,0:T(8,128)(2,1)S(1)}, bf16[64,640]{1,0:T(8,128)(2,1)S(1)}, u32[]{:S(2)}, u32[]{:S(2)}) collective-permute-start(bf16[64,640]{1,0:T(8,128)(2,1)S(1)} %shard_map.127.refs_0_), channel_id=1, source_target_pairs={{0,16},{16,32},{32,48},{48,0},{1,17},{17,33},{33,49},{49,1},{2,18}... | collective-permute-start | bytes 245768 | tf_op jit(solution)/shard_map/ppermute | solution.py:28
  17.9 12.1 %collective-permute-start.2 = (bf16[64,640]{1,0:T(8,128)(2,1)S(1)}, bf16[64,640]{1,0:T(8,128)(2,1)S(1)}, u32[]{:S(2)}, u32[]{:S(2)}) collective-permute-start(bf16[64,640]{1,0:T(8,128)(2,1)S(1)} %shard_map.127.refs_0_), channel_id=1, source_target_pairs={{0,48},{16,0},{32,16},{48,32},{1,49},{17,1},{33,17},{49,33},{2,50}... | collective-permute-start | bytes 245768 | tf_op jit(solution)/shard_map/ppermute | solution.py:28
  30.0 1.7 %collective-permute-start.5 = (bf16[256,640]{1,0:T(8,128)(2,1)S(1)}, bf16[256,640]{1,0:T(8,128)(2,1)S(1)}, u32[]{:S(2)}, u32[]{:S(2)}) collective-permute-start(bf16[256,640]{1,0:T(8,128)(2,1)S(1)} %collective-permute-done.3.refs_6_), channel_id=1, source_target_pairs={{0,4},{4,0},{1,5},{5,1},{2,6},{6,2},{3,7},{7,3},{8,12},{12,8},{9,1... | collective-permute-start | bytes 983048 | tf_op jit(solution)/shard_map/ppermute | solution.py:32
  34.2 5.9 %collective-permute-start.6 = (f32[16,256]{1,0:T(8,128)S(1)}, f32[16,256]{1,0:T(8,128)S(1)}, u32[]{:S(2)}, u32[]{:S(2)}) collective-permute-start(f32[16,256]{1,0:T(8,128)S(1)} %shard_map.129.refs_8_), channel_id=1, source_target_pairs={{0,16},{16,32},{32,48},{48,0},{1,17},{17,33},{33,49},{49,1},{2,18}... | collective-permute-start | bytes 49160 | tf_op jit(solution)/shard_map/ppermute | solution.py:28
  35.4 7.6 %collective-permute-start.7 = (f32[16,256]{1,0:T(8,128)S(1)}, f32[16,256]{1,0:T(8,128)S(1)}, u32[]{:S(2)}, u32[]{:S(2)}) collective-permute-start(f32[16,256]{1,0:T(8,128)S(1)} %shard_map.129.refs_8_), channel_id=1, source_target_pairs={{0,32},{16,48},{32,0},{48,16},{1,33},{17,49},{33,1},{49,17},{2,34}... | collective-permute-start | bytes 49160 | tf_op jit(solution)/shard_map/ppermute | solution.py:28
  38.1 4.9 %collective-permute-start.8 = (f32[16,256]{1,0:T(8,128)S(1)}, f32[16,256]{1,0:T(8,128)S(1)}, u32[]{:S(2)}, u32[]{:S(2)}) collective-permute-start(f32[16,256]{1,0:T(8,128)S(1)} %shard_map.129.refs_8_), channel_id=1, source_target_pairs={{0,48},{16,0},{32,16},{48,32},{1,49},{17,1},{33,17},{49,33},{2,50}... | collective-permute-start | bytes 49160 | tf_op jit(solution)/shard_map/ppermute | solution.py:28
  50.2 0.9 copy-start.8
  51.1 0.9 copy-start.10
  53.2 3.3 %collective-permute-start.9 = (bf16[512,640]{1,0:T(8,128)(2,1)}, bf16[512,640]{1,0:T(8,128)(2,1)S(1)}, u32[]{:S(2)}, u32[]{:S(2)}) collective-permute-start(bf16[512,640]{1,0:T(8,128)(2,1)} %get-tuple-element.44), channel_id=1, source_target_pairs={{0,4},{4,0},{1,5},{5,1},{2,6},{6,2},{3,7},{7,3},{8,12},{12,8},{9,1... | collective-permute-start | bytes 1966088 | tf_op jit(solution)/shard_map/ppermute | solution.py:32
  53.2 3.3 %copy-start.9 = (f32[256,640]{1,0:T(8,128)S(1)}, f32[256,640]{1,0:T(8,128)}, u32[]{:S(2)}) copy-start(f32[256,640]{1,0:T(8,128)} %copy-done.8) | copy-start | bytes 1966084
  56.5 1.6 %copy-start.19 = (bf16[64,640]{1,0:T(8,128)(2,1)S(1)}, bf16[64,640]{1,0:T(8,128)(2,1)}, u32[]{:S(2)}) copy-start(bf16[64,640]{1,0:T(8,128)(2,1)} %copy-done.18) | copy-start | bytes 245764
  56.5 4.5 %copy-start.17 = (bf16[64,640]{1,0:T(8,128)(2,1)S(1)}, bf16[64,640]{1,0:T(8,128)(2,1)}, u32[]{:S(2)}) copy-start(bf16[64,640]{1,0:T(8,128)(2,1)} %copy-done.16) | copy-start | bytes 245764
  56.6 19.7 %copy-start.11 = (f32[256,640]{1,0:T(8,128)S(1)}, f32[256,640]{1,0:T(8,128)}, u32[]{:S(2)}) copy-start(f32[256,640]{1,0:T(8,128)} %copy-done.10) | copy-start | bytes 1966084
  56.6 19.7 %collective-permute-start.10 = (bf16[256,640]{1,0:T(8,128)(2,1)S(1)}, bf16[256,640]{1,0:T(8,128)(2,1)S(1)}, u32[]{:S(2)}, u32[]{:S(2)}) collective-permute-start(bf16[256,640]{1,0:T(8,128)(2,1)S(1)} %add_convert_fusion), channel_id=1, source_target_pairs={{0,8},{8,0},{1,9},{9,1},{2,10},{10,2},{3,11},{11,3},{4,12},{12,4},... | collective-permute-start | bytes 983048 | tf_op jit(solution)/shard_map/ppermute | solution.py:32
  58.1 14.4 %collective-permute-start.11 = (bf16[64,640]{1,0:T(8,128)(2,1)S(1)}, bf16[64,640]{1,0:T(8,128)(2,1)S(1)}, u32[]{:S(2)}, u32[]{:S(2)}) collective-permute-start(bf16[64,640]{1,0:T(8,128)(2,1)S(1)} %copy-done.19), channel_id=1, source_target_pairs={{0,32},{16,48},{32,0},{48,16},{1,33},{17,49},{33,1},{49,17},{2,34}... | collective-permute-start | bytes 245768 | tf_op jit(solution)/shard_map/ppermute | solution.py:28
  61.0 11.5 %collective-permute-start.12 = (bf16[64,640]{1,0:T(8,128)(2,1)S(1)}, bf16[64,640]{1,0:T(8,128)(2,1)S(1)}, u32[]{:S(2)}, u32[]{:S(2)}) collective-permute-start(bf16[64,640]{1,0:T(8,128)(2,1)S(1)} %copy-done.17), channel_id=1, source_target_pairs={{0,48},{16,0},{32,16},{48,32},{1,49},{17,1},{33,17},{49,33},{2,50}... | collective-permute-start | bytes 245768 | tf_op jit(solution)/shard_map/ppermute | solution.py:28
  64.5 11.8 %collective-permute-start.13 = (bf16[64,640]{1,0:T(8,128)(2,1)S(1)}, bf16[64,640]{1,0:T(8,128)(2,1)S(1)}, u32[]{:S(2)}, u32[]{:S(2)}) collective-permute-start(bf16[64,640]{1,0:T(8,128)(2,1)S(1)} %get-tuple-element.53), channel_id=1, source_target_pairs={{0,16},{16,32},{32,48},{48,0},{1,17},{17,33},{33,49},{49,1},{2,18}... | collective-permute-start | bytes 245768 | tf_op jit(solution)/shard_map/ppermute | solution.py:28
  64.6 12.2 %collective-permute-start.14 = (bf16[640,384]{1,0:T(8,128)(2,1)S(1)}, bf16[640,384]{1,0:T(8,128)(2,1)S(1)}, u32[]{:S(2)}, u32[]{:S(2)}) collective-permute-start(bf16[640,384]{1,0:T(8,128)(2,1)S(1)} %get-tuple-element.74), channel_id=1, source_target_pairs={{0,4},{4,0},{1,5},{5,1},{2,6},{6,2},{3,7},{7,3},{8,12},{12,8},{9,1... | collective-permute-start | bytes 1474568 | tf_op jit(solution)/shard_map/ppermute | solution.py:32
  76.4 13.2 %copy-start.3 = (bf16[1280,320]{0,1:T(8,128)(2,1)S(1)}, bf16[1280,320]{0,1:T(8,128)(2,1)}, u32[]{:S(2)}) copy-start(bf16[1280,320]{0,1:T(8,128)(2,1)} %param.12) | copy-start | bytes 2457604
  76.5 2.1 %collective-permute-start.15 = (bf16[320,640]{1,0:T(8,128)(2,1)S(1)}, bf16[320,640]{1,0:T(8,128)(2,1)S(1)}, u32[]{:S(2)}, u32[]{:S(2)}) collective-permute-start(bf16[320,640]{1,0:T(8,128)(2,1)S(1)} %shard_map.131.y_ref), channel_id=1, source_target_pairs={{0,4},{4,0},{1,5},{5,1},{2,6},{6,2},{3,7},{7,3},{8,12},{12,8},{9,1... | collective-permute-start | bytes 1228808 | tf_op jit(solution)/shard_map/ppermute | solution.py:32
  80.6 0.9 copy-start.4
  81.5 0.7 copy-start.12
  82.2 11.3 %collective-permute-start.19 = (bf16[160,640]{1,0:T(8,128)(2,1)}, bf16[160,640]{1,0:T(8,128)(2,1)}, u32[]{:S(2)}, u32[]{:S(2)}) collective-permute-start(bf16[160,640]{1,0:T(8,128)(2,1)} %get-tuple-element.61), channel_id=1, source_target_pairs={{0,128},{64,192},{128,0},{192,64},{1,129},{65,193},{129,1},{193,65... | collective-permute-start | bytes 614408 | tf_op jit(solution)/shard_map/ppermute | solution.py:28
  85.2 10.3 %collective-permute-start.20 = (bf16[160,640]{1,0:T(8,128)(2,1)}, bf16[160,640]{1,0:T(8,128)(2,1)}, u32[]{:S(2)}, u32[]{:S(2)}) collective-permute-start(bf16[160,640]{1,0:T(8,128)(2,1)} %get-tuple-element.62), channel_id=1, source_target_pairs={{0,64},{64,128},{128,192},{192,0},{1,65},{65,129},{129,193},{193,1... | collective-permute-start | bytes 614408 | tf_op jit(solution)/shard_map/ppermute | solution.py:28
  85.8 10.2 %collective-permute-start.21 = (bf16[160,640]{1,0:T(8,128)(2,1)}, bf16[160,640]{1,0:T(8,128)(2,1)}, u32[]{:S(2)}, u32[]{:S(2)}) collective-permute-start(bf16[160,640]{1,0:T(8,128)(2,1)} %get-tuple-element.63), channel_id=1, source_target_pairs={{0,192},{64,0},{128,64},{192,128},{1,193},{65,1},{129,65},{193,129... | collective-permute-start | bytes 614408 | tf_op jit(solution)/shard_map/ppermute | solution.py:28
  88.5 16.7 %collective-permute-start.23 = (bf16[320,640]{1,0:T(8,128)(2,1)}, bf16[320,640]{1,0:T(8,128)(2,1)S(1)}, u32[]{:S(2)}, u32[]{:S(2)}) collective-permute-start(bf16[320,640]{1,0:T(8,128)(2,1)} %get-tuple-element.65), channel_id=1, source_target_pairs={{0,8},{8,0},{1,9},{9,1},{2,10},{10,2},{3,11},{11,3},{4,12},{12,4},... | collective-permute-start | bytes 1228808 | tf_op jit(solution)/shard_map/ppermute | solution.py:32
  89.6 6.4 %copy-start.13 = (f32[160,640]{1,0:T(8,128)S(1)}, f32[160,640]{1,0:T(8,128)}, u32[]{:S(2)}) copy-start(f32[160,640]{1,0:T(8,128)} %copy-done.12) | copy-start | bytes 1228804
  91.2 8.9 %collective-permute-start.16 = (bf16[320,320]{1,0:T(8,128)(2,1)S(1)}, bf16[320,320]{1,0:T(8,128)(2,1)S(1)}, u32[]{:S(2)}, u32[]{:S(2)}) collective-permute-start(bf16[320,320]{1,0:T(8,128)(2,1)S(1)} %get-tuple-element.57), channel_id=1, source_target_pairs={{0,2},{1,3},{2,0},{3,1},{4,6},{5,7},{6,4},{7,5},{8,10},{9,11},{10,... | collective-permute-start | bytes 614408 | tf_op jit(solution)/shard_map/ppermute | solution.py:28
  93.5 11.5 %collective-permute-start.17 = (bf16[320,320]{1,0:T(8,128)(2,1)S(1)}, bf16[320,320]{1,0:T(8,128)(2,1)S(1)}, u32[]{:S(2)}, u32[]{:S(2)}) collective-permute-start(bf16[320,320]{1,0:T(8,128)(2,1)S(1)} %get-tuple-element.58), channel_id=1, source_target_pairs={{0,1},{1,2},{2,3},{3,0},{4,5},{5,6},{6,7},{7,4},{8,9},{9,10},{10,1... | collective-permute-start | bytes 614408 | tf_op jit(solution)/shard_map/ppermute | solution.py:28
  95.6 9.5 %collective-permute-start.18 = (bf16[320,320]{1,0:T(8,128)(2,1)S(1)}, bf16[320,320]{1,0:T(8,128)(2,1)S(1)}, u32[]{:S(2)}, u32[]{:S(2)}) collective-permute-start(bf16[320,320]{1,0:T(8,128)(2,1)S(1)} %get-tuple-element.59), channel_id=1, source_target_pairs={{0,3},{1,0},{2,1},{3,2},{4,7},{5,4},{6,5},{7,6},{8,11},{9,8},{10,9... | collective-permute-start | bytes 614408 | tf_op jit(solution)/shard_map/ppermute | solution.py:28
  97.3 8.0 %copy-start.5 = (f32[320,640]{1,0:T(8,128)S(1)}, f32[320,640]{1,0:T(8,128)}, u32[]{:S(2)}) copy-start(f32[320,640]{1,0:T(8,128)} %copy-done.4) | copy-start | bytes 2457604
  97.3 11.5 %collective-permute-start.22 = (bf16[80,640]{1,0:T(8,128)(2,1)S(1)}, bf16[80,640]{1,0:T(8,128)(2,1)S(1)}, u32[]{:S(2)}, u32[]{:S(2)}) collective-permute-start(bf16[80,640]{1,0:T(8,128)(2,1)S(1)} %slice.115), channel_id=1, source_target_pairs={{0,8},{8,0},{1,9},{9,1},{2,10},{10,2},{3,11},{11,3},{4,12},{12,4},... | collective-permute-start | bytes 307208 | tf_op jit(solution)/shard_map/ppermute | solution.py:32
  105.4 7.4 %collective-permute-start.24 = (bf16[80,640]{1,0:T(8,128)(2,1)S(1)}, bf16[80,640]{1,0:T(8,128)(2,1)S(1)}, u32[]{:S(2)}, u32[]{:S(2)}) collective-permute-start(bf16[80,640]{1,0:T(8,128)(2,1)S(1)} %get-tuple-element.76), channel_id=1, source_target_pairs={{0,128},{64,192},{128,0},{192,64},{1,129},{65,193},{129,1},{193,65... | collective-permute-start | bytes 307208 | tf_op jit(solution)/shard_map/ppermute | solution.py:28
  105.5 8.2 %collective-permute-start.25 = (bf16[80,640]{1,0:T(8,128)(2,1)S(1)}, bf16[80,640]{1,0:T(8,128)(2,1)S(1)}, u32[]{:S(2)}, u32[]{:S(2)}) collective-permute-start(bf16[80,640]{1,0:T(8,128)(2,1)S(1)} %get-tuple-element.78), channel_id=1, source_target_pairs={{0,64},{64,128},{128,192},{192,0},{1,65},{65,129},{129,193},{193,1... | collective-permute-start | bytes 307208 | tf_op jit(solution)/shard_map/ppermute | solution.py:28
  106.6 7.0 %collective-permute-start.26 = (bf16[80,640]{1,0:T(8,128)(2,1)S(1)}, bf16[80,640]{1,0:T(8,128)(2,1)S(1)}, u32[]{:S(2)}, u32[]{:S(2)}) collective-permute-start(bf16[80,640]{1,0:T(8,128)(2,1)S(1)} %get-tuple-element.77), channel_id=1, source_target_pairs={{0,192},{64,0},{128,64},{192,128},{1,193},{65,1},{129,65},{193,129... | collective-permute-start | bytes 307208 | tf_op jit(solution)/shard_map/ppermute | solution.py:28
  113.8 8.8 %collective-permute-start.27 = (bf16[20,1280]{1,0:T(8,128)(2,1)S(1)}, bf16[20,1280]{1,0:T(8,128)(2,1)S(1)}, u32[]{:S(2)}, u32[]{:S(2)}) collective-permute-start(bf16[20,1280]{1,0:T(8,128)(2,1)S(1)} %get-tuple-element.79), channel_id=1, source_target_pairs={{0,32},{16,48},{32,0},{48,16},{1,33},{17,49},{33,1},{49,17},{2,34}... | collective-permute-start | bytes 153608 | tf_op jit(solution)/shard_map/ppermute | solution.py:28
  115.7 7.1 %collective-permute-start.28 = (bf16[20,1280]{1,0:T(8,128)(2,1)S(1)}, bf16[20,1280]{1,0:T(8,128)(2,1)S(1)}, u32[]{:S(2)}, u32[]{:S(2)}) collective-permute-start(bf16[20,1280]{1,0:T(8,128)(2,1)S(1)} %get-tuple-element.81), channel_id=1, source_target_pairs={{0,16},{16,32},{32,48},{48,0},{1,17},{17,33},{33,49},{49,1},{2,18}... | collective-permute-start | bytes 153608 | tf_op jit(solution)/shard_map/ppermute | solution.py:28
  118.4 6.1 %collective-permute-start.29 = (bf16[20,1280]{1,0:T(8,128)(2,1)S(1)}, bf16[20,1280]{1,0:T(8,128)(2,1)S(1)}, u32[]{:S(2)}, u32[]{:S(2)}) collective-permute-start(bf16[20,1280]{1,0:T(8,128)(2,1)S(1)} %get-tuple-element.80), channel_id=1, source_target_pairs={{0,48},{16,0},{32,16},{48,32},{1,49},{17,1},{33,17},{49,33},{2,50}... | collective-permute-start | bytes 153608 | tf_op jit(solution)/shard_map/ppermute | solution.py:28
  (2 other events, 1.3 us)
